TPU v7x, 32 devices: a whole 2x2x4 slice. The times are simulated.
32 devices in a mesh: image: 4 (over x, core), space: 8 (over z, y).
Axes of the slice: x: 2, y: 2, z: 4, core: 2. Of those that a mesh axis runs over, the one named last changes fastest.
Arguments:
- positions: float32 [8, 3, 2048], P('image', None, 'space'), may hold values from -6 to 6
- velocity: float32 [8, 3, 2048], P('image', None, 'space'), may hold values from -4 to 4
- start_state: float32 [3, 2048], P(None, 'space'), may hold values from -6 to 6
- end_state: float32 [3, 2048], P(None, 'space'), may hold values from -6 to 6
- neighbours: int32 [8, 16, 2048], P('image', None, 'space'), may hold values from 0 to 511, as said below
- counts: int32 [8, 2048], P('image', 'space'), may hold values from 1 to 16, as said below
- climb_index: int32 [1], replicated, may hold values from 0 to 7
- radial_a1: float32 [8, 64], replicated, may hold values from -2 to 2
- radial_b1: float32 [64, 128], replicated, may hold values from -0.75 to 0.75
- mix_first: float32 [384, 128], replicated, may hold values from -0.5 to 0.5
- read_first: float32 [128], replicated, may hold values from -0.5 to 0.5
- radial_a2: float32 [8, 64], replicated, may hold values from -2 to 2
- radial_b2: float32 [64, 128], replicated, may hold values from -0.75 to 0.75
- mix_second: float32 [384, 128], replicated, may hold values from -0.5 to 0.5
- read_second: float32 [128], replicated, may hold values from -0.5 to 0.5
Outputs:
- neb_force: float32 [8, 3, 2048], P('image', None, 'space')
- velocity_next: float32 [8, 3, 2048], P('image', None, 'space')
- position_next: float32 [8, 3, 2048], P('image', None, 'space')
- image_energy: float32 [8], P('image')
Inputs may be any that keep to these rules, and one draw needn't show every extreme that they name: `neighbours`: A slab's extended atoms are, in order, the last 128 atoms of the slab below, its own 256 atoms, and the first 128 atoms of the slab above; the first and last slabs are beside each other. `counts`: atoms in the middle of the image have a higher least number of live neighbours than those at its ends.
All inputs are finite; a program needn't handle non-finite values.
Results may differ from a plain program's by a relative error of at most 0.0003.
Values sent between devices are 32-bit elements; how exact they have to be, the bound alone decides.
A program may use at most 64 MiB of HBM per device.

v0:
```python
import math

import jax
import jax.numpy as jnp
from jax import lax
from jax.sharding import PartitionSpec as P

highest = lax.Precision.HIGHEST


def padded(cells, sides, width, closed):
    for axis, dim in sides:
        count = lax.axis_size(axis)
        ends = count if closed else count - 1
        head = lax.slice_in_dim(cells, 0, width, axis=dim)
        tail = lax.slice_in_dim(cells, cells.shape[dim] - width, cells.shape[dim], axis=dim)
        cells = jnp.concatenate(
            [
                lax.ppermute(tail, axis, [(i, (i + 1) % count) for i in range(ends)]),
                cells,
                lax.ppermute(head, axis, [((i + 1) % count, i) for i in range(ends)]),
            ],
            axis=dim,
        )
    return cells


def harmonics(unit):
    ux = unit[0]
    uy = unit[1]
    uz = unit[2]
    return jnp.stack(
        [
            jnp.ones_like(ux),
            ux,
            uy,
            uz,
            ux * uy,
            uy * uz,
            ux * uz,
            0.5 * (ux * ux - uy * uy),
            (3.0 * uz * uz - 1.0) / (2.0 * math.sqrt(3.0)),
        ]
    )


def layer_out(center, nb_pos, live_mask, radial_a, radial_b, mixing, nb_feat):
    offset = nb_pos - center[:, None, :]
    length = jnp.sqrt(jnp.sum(offset * offset, axis=0) + 1.0)
    angular = harmonics(offset / length[None])
    centres = 0.5 * jnp.arange(radial_a.shape[0]).astype(center.dtype)
    spread = length[None] - centres[:, None, None]
    basis = jnp.exp(-spread * spread / 0.5)
    hidden = jax.nn.silu(jnp.einsum("bka,bh->hka", basis, radial_a, precision=highest))
    radial = jnp.einsum("hka,hc->cka", hidden, radial_b, precision=highest) * live_mask[None]
    if nb_feat is not None:
        radial = radial * nb_feat
    moments = jnp.einsum("cka,lka->cla", radial, angular, precision=highest) / live_mask.shape[0]
    invariants = jnp.concatenate(
        [
            moments[:, 0],
            jnp.sum(moments[:, 1:4] * moments[:, 1:4], axis=1),
            jnp.sum(moments[:, 4:9] * moments[:, 4:9], axis=1),
        ],
        axis=0,
    )
    return jax.nn.silu(jnp.einsum("fa,fc->ca", invariants, mixing, precision=highest))


def own_part(grad_ext, atoms):
    ghost = (grad_ext.shape[-1] - atoms) // 2
    return grad_ext[..., ghost : ghost + atoms]


def ghost_parts(grad_ext, atoms):
    ghost = (grad_ext.shape[-1] - atoms) // 2
    return jnp.concatenate([grad_ext[..., :ghost], grad_ext[..., ghost + atoms :]], axis=-1)


def add_returned(own, returned):
    ghost = returned.shape[-1] // 4
    atoms = own.shape[-1]
    leading = [(0, 0)] * (own.ndim - 1)
    lower = jnp.pad(returned[..., :ghost], leading + [(0, atoms - ghost)])
    upper = jnp.pad(returned[..., 3 * ghost :], leading + [(atoms - ghost, 0)])
    return own + lower + upper


def local(
    positions,
    velocity,
    start_state,
    end_state,
    neighbours,
    counts,
    climb_index,
    radial_a1,
    radial_b1,
    mix_first,
    read_first,
    radial_a2,
    radial_b2,
    mix_second,
    read_second,
):
    atoms = positions.shape[2]
    ghost = atoms // 2
    img_count = positions.shape[0]
    slots = lax.broadcasted_iota(jnp.int32, neighbours.shape, 1)
    live_all = (slots < counts[:, None, :]).astype(jnp.float32)

    def first_layer(ext_pos, nb_idx, live_mask):
        center = ext_pos[:, ghost : ghost + atoms]
        return layer_out(
            center, ext_pos[:, nb_idx], live_mask, radial_a1, radial_b1, mix_first, None
        )

    def second_energy(ext_pos, ext_feat, nb_idx, live_mask):
        center = ext_pos[:, ghost : ghost + atoms]
        second = layer_out(
            center,
            ext_pos[:, nb_idx],
            live_mask,
            radial_a2,
            radial_b2,
            mix_second,
            ext_feat[:, nb_idx],
        )
        return jnp.sum(read_second[:, None] * second)

    def one_image(items):
        image_pos, nb_idx, live_mask = items
        ext_pos = padded(image_pos, (("space", 1),), ghost, True)

        def layer_one(pos_arg):
            return first_layer(pos_arg, nb_idx, live_mask)

        feat_own, back_one = jax.vjp(layer_one, ext_pos)
        ext_feat = padded(feat_own, (("space", 1),), ghost, True)

        def layer_two(pos_arg, feat_arg):
            return second_energy(pos_arg, feat_arg, nb_idx, live_mask)

        energy_two, back_two = jax.vjp(layer_two, ext_pos, ext_feat)
        grad_pos2, grad_feat = back_two(jnp.ones_like(energy_two))
        returned = padded(ghost_parts(grad_feat, atoms), (("space", 1),), ghost, True)
        feat_cot = add_returned(own_part(grad_feat, atoms), returned) + read_first[:, None]
        grad_total = back_one(feat_cot)[0] + grad_pos2
        back_pos = padded(ghost_parts(grad_total, atoms), (("space", 1),), ghost, True)
        image_force = -add_returned(own_part(grad_total, atoms), back_pos)
        energy = jnp.sum(read_first[:, None] * feat_own) + energy_two
        return (image_force, energy)

    forces, energies = lax.map(one_image, (positions, neighbours, live_all))
    chain = padded(positions, (("image", 0),), 1, False)
    first_dev = lax.axis_index("image") == 0
    last_dev = lax.axis_index("image") == lax.axis_size("image") - 1
    prev_pos = jnp.concatenate(
        [jnp.where(first_dev, start_state, chain[0])[None], chain[1:img_count]], axis=0
    )
    next_pos = jnp.concatenate(
        [chain[2 : img_count + 1], jnp.where(last_dev, end_state, chain[img_count + 1])[None]],
        axis=0,
    )
    spread = next_pos - prev_pos
    ahead = next_pos - positions
    behind = positions - prev_pos
    ahead_loc = jnp.sum(ahead * ahead, axis=(1, 2))
    behind_loc = jnp.sum(behind * behind, axis=(1, 2))
    spread_loc = jnp.sum(spread * spread, axis=(1, 2))
    project_loc = jnp.sum(forces * spread, axis=(1, 2))
    dist_ahead, dist_behind, spread_sq, energy_sum, projected = lax.psum(
        (ahead_loc, behind_loc, spread_loc, energies, project_loc), "space"
    )
    norm_path = jnp.sqrt(spread_sq + 1e-06)
    tangent = spread / norm_path[:, None, None]
    along = projected / norm_path
    spring = 5.0 * (jnp.sqrt(dist_ahead) - jnp.sqrt(dist_behind))
    image_ids = lax.axis_index("image") * img_count + jnp.arange(img_count)
    climbing = (image_ids == climb_index[0]).astype(jnp.float32)
    coef = -(1.0 + climbing) * along + (1.0 - climbing) * spring
    neb_force = forces + coef[:, None, None] * tangent
    vel_sq, force_sq = lax.psum(
        (jnp.sum(velocity * velocity), jnp.sum(neb_force * neb_force)), ("image", "space")
    )
    velocity_next = (
        0.9 * velocity + 0.1 * jnp.sqrt(vel_sq / (force_sq + 1e-06)) * neb_force + 0.1 * neb_force
    )
    position_next = positions + 0.1 * velocity_next
    image_energy = energy_sum / (atoms * lax.axis_size("space"))
    return (neb_force, velocity_next, position_next, image_energy)


def solution(mesh):
    in_specs = (
        P("image", None, "space"),
        P("image", None, "space"),
        P(None, "space"),
        P(None, "space"),
        P("image", None, "space"),
        P("image", "space"),
        P(),
        P(),
        P(),
        P(),
        P(),
        P(),
        P(),
        P(),
        P(),
    )
    out_specs = (
        P("image", None, "space"),
        P("image", None, "space"),
        P("image", None, "space"),
        P("image"),
    )
    return jax.shard_map(local, mesh=mesh, in_specs=in_specs, out_specs=out_specs, check_vma=False)
```

profile of v0, /device:TPU:0, one launch (start us, length us, event | category | flops | bytes accessed | tf_op | source)
XLA Modules:
  0.0 480.3 jit_solution(6269319939091604186)
XLA Ops:
  2.6 2.3 collective-permute-start.9
  11.5 404.8 %while.14 = (s32[]{:T(128)}, f32[2,3,256]{2,1,0:T(4,128)}, f32[2]{0:T(128)}, f32[2,3,256]{2,1,0:T(4,128)}, s32[2,16,256]{2,1,0:T(8,128)}, /*index=5*/f32[8,64]{1...) while((s32[]{:T(128)}, f32[2,3,256]{2,1,0:T(4,128)}, ...), condition=%wide.region_17.18_spmd, body=%wide.region_0.17_spmd.sunk | while | flops 2677775104 | bytes 138035984 | solution.py:154
  12.2 5.4 %collective-permute-start = (f32[3,128]{1,0:T(4,128)S(1)}, f32[3,128]{1,0:T(4,128)S(1)}, u32[]{:S(2)}, u32[]{:S(2)}) collective-permute-start(f32[3,128]{1,0:T(4,128)S(1)} %get-tuple-element.520), channel_id=1, source_target_pairs={{1,0},{2,1},{3,2},{4,3},{5,4},{6,5},{7,6},{0,7},{9,8},{10,9},{11,1... | collective-permute-start | bytes 4616 | tf_op jit(solution)/shard_map/while/body/eval_jaxpr/ppermute | solution.py:21
  19.1 4.8 collective-permute-done.1
  24.0 10.8 %gather_fusion = f32[4096,3]{1,0:T(8,128)S(1)} fusion(f32[3,512]{0,1:T(8,128)S(1)} %copy.334, s32[4096]{0:T(1024)S(1)} %broadcast_clamp_fusion.2), kind=kCustom, calls=%fused_computation.clone.1 | custom fusion | bytes 114688 | tf_op jit(solution)/shard_map/while/body/eval_jaxpr/jvp()/gather | solution.py:115
  38.6 3.9 multiply_bitcast_fusion.6
  42.6 4.5 multiply_bitcast_fusion.7
  48.2 2.3 multiply_reduce_fusion.26
  54.8 3.3 collective-permute-done.3
  58.1 15.4 %gather_fusion.1 = f32[4096,128]{1,0:T(8,128)} fusion(f32[128,512]{0,1:T(8,128)S(1)} %pad_maximum_fusion.7, s32[4096]{0:T(1024)} %copy-done.16), kind=kCustom, calls=%fused_computation.1.clone.1 | custom fusion | bytes 4210688 | tf_op jit(solution)/shard_map/while/body/eval_jaxpr/jvp()/gather | solution.py:127
  73.6 6.2 %bitcast_multiply_fusion.11 = (f32[128,16,256]{0,2,1:T(8,128)S(1)}, f32[16,256,128]{2,1,0:T(8,128)}) fusion(f32[128,16,256]{0,2,1:T(8,128)} %bitcast.269, f32[16,256]{1,0:T(8,128)S(1)} %dynamic-slice_bitcast_fusion.5, f32[64,128]{1,0:T(8,128)} %get-tuple-element.600, f32[64,16,256]{2,0,1:T(8,128)S(1)} %convolution_bitcast_fusion.12), kind=kOutput, calls=%fused_computation.19.clone.1 | convolution fusion | flops 404750336 | bytes 7389184 | tf_op jit(solution)/shard_map/while/body/eval_jaxpr/jvp(hka,hc->cka)/dot_general | solution.py:55
  79.8 4.5 multiply_bitcast_fusion.8
  87.3 6.2 %fusion.289 = f32[256,9,16]{2,1,0:T(8,128)} fusion(f32[128,16,256]{0,2,1:T(8,128)S(1)} %get-tuple-element.528, f32[128,1,256]{0,1,2:T(1,128)S(1)} %bitcast.277, f32[128,3,256]{0,1,2:T(4,128)S(1)} %slice_multiply_fusion.12, f32[128,5,256]{0,1,2:T(8,128)S(1)} %slice_multiply_fusion.13), kind=kOutput, calls=%fused_computation.25.clone.1 | convolution fusion | flops 58097664 | bytes 3424256 | tf_op jit(solution)/shard_map/while/body/eval_jaxpr/transpose(jvp(cka,lka->cla))/dot_general | solution.py:58
  93.4 4.6 fusion.283
  100.2 4.8 %fusion.284 = f32[64,16,256]{2,0,1:T(8,128)S(1)} fusion(f32[128,16,256]{0,2,1:T(8,128)} %bitcast.270, f32[256,128,16]{1,2,0:T(8,128)} %fusion.283, f32[16,256]{1,0:T(8,128)S(1)} %dynamic-slice_bitcast_fusion.5, f32[64,128]{1,0:T(8,128)S(1)} %copy-done.17), kind=kOutput, calls=%fused_computation.35.clone.1 | convolution fusion | flops 403701760 | bytes 5292032 | tf_op jit(solution)/shard_map/while/body/eval_jaxpr/transpose(jvp(hka,hc->cka))/dot_general | solution.py:55
  105.0 2.4 bitcast_multiply_fusion.12
  109.1 22.7 %scatter_custom_fusion.9 = f32[128,512]{0,1:T(8,128)S(1)} fusion(s32[4096]{0:T(1024)S(1)} %bitcast.284, f32[4096,128]{1,0:T(8,128)} %bitcast.274, f32[]{:T(128)} %constant.107.clone.38..sunk), kind=kCustom, calls=%fused_computation.131.clone.1 | custom fusion | flops 524288 | bytes 262656 | tf_op jit(solution)/shard_map/while/body/eval_jaxpr/transpose(jvp())/scatter-add | solution.py:127
  131.9 2.2 collective-permute-start.5
  136.1 3.0 collective-permute-done.5
  141.1 4.3 fusion.293
  145.4 6.2 %fusion.288 = f32[256,9,16]{2,1,0:T(8,128)} fusion(f32[128,16,256]{0,2,1:T(8,128)S(1)} %copy-done.4, f32[128,1,256]{0,1,2:T(1,128)S(1)} %bitcast.276, f32[128,3,256]{0,1,2:T(4,128)S(1)} %slice_multiply_fusion.14, f32[128,5,256]{0,1,2:T(8,128)S(1)} %slice_multiply_fusion.15), kind=kOutput, calls=%fused_computation.29.clone.1 | convolution fusion | flops 58097664 | bytes 3424256 | tf_op jit(solution)/shard_map/while/body/eval_jaxpr/transpose(jvp(cka,lka->cla))/dot_general | solution.py:58
  151.6 2.3 copy.338
  154.8 3.8 fusion.294
  162.9 22.8 %scatter_fusion = f32[3,512]{0,1:T(8,128)S(1)} fusion(f32[3,512]{0,1:T(8,128)S(1)} %pad.328, s32[4096]{0:T(1024)S(1)} %bitcast.285, f32[4096,3]{1,0:T(8,128)} %bitcast.272), kind=kCustom, calls=%fused_computation.3.clone.1 | custom fusion | flops 12288 | bytes 163840 | tf_op jit(solution)/shard_map/while/body/eval_jaxpr/transpose(jvp())/scatter-add | solution.py:115
  185.7 22.5 %scatter_fusion.1 = f32[3,512]{0,1:T(8,128)S(1)} fusion(f32[3,512]{0,1:T(8,128)S(1)} %pad.329, s32[4096]{0:T(1024)S(1)} %bitcast.286, f32[4096,3]{1,0:T(8,128)S(1)} %bitcast.271), kind=kCustom, calls=%fused_computation.4.clone.1 | custom fusion | flops 12288 | bytes 163840 | tf_op jit(solution)/shard_map/while/body/eval_jaxpr/transpose(jvp())/scatter-add | solution.py:122
  220.4 2.7 collective-permute-done.1
  223.4 10.8 %gather_fusion = f32[4096,3]{1,0:T(8,128)S(1)} fusion(f32[3,512]{0,1:T(8,128)S(1)} %copy.334, s32[4096]{0:T(1024)S(1)} %broadcast_clamp_fusion.2), kind=kCustom, calls=%fused_computation.clone.1 | custom fusion | bytes 114688 | tf_op jit(solution)/shard_map/while/body/eval_jaxpr/jvp()/gather | solution.py:115
  238.0 3.9 multiply_bitcast_fusion.6
  241.9 4.5 multiply_bitcast_fusion.7
  253.9 2.8 collective-permute-done.3
  256.6 15.4 %gather_fusion.1 = f32[4096,128]{1,0:T(8,128)} fusion(f32[128,512]{0,1:T(8,128)S(1)} %pad_maximum_fusion.7, s32[4096]{0:T(1024)} %copy-done.16), kind=kCustom, calls=%fused_computation.1.clone.1 | custom fusion | bytes 4210688 | tf_op jit(solution)/shard_map/while/body/eval_jaxpr/jvp()/gather | solution.py:127
  272.1 6.2 %bitcast_multiply_fusion.11 = (f32[128,16,256]{0,2,1:T(8,128)S(1)}, f32[16,256,128]{2,1,0:T(8,128)}) fusion(f32[128,16,256]{0,2,1:T(8,128)} %bitcast.269, f32[16,256]{1,0:T(8,128)S(1)} %dynamic-slice_bitcast_fusion.5, f32[64,128]{1,0:T(8,128)} %get-tuple-element.600, f32[64,16,256]{2,0,1:T(8,128)S(1)} %convolution_bitcast_fusion.12), kind=kOutput, calls=%fused_computation.19.clone.1 | convolution fusion | flops 404750336 | bytes 7389184 | tf_op jit(solution)/shard_map/while/body/eval_jaxpr/jvp(hka,hc->cka)/dot_general | solution.py:55
  278.3 4.5 multiply_bitcast_fusion.8
  285.8 6.2 %fusion.289 = f32[256,9,16]{2,1,0:T(8,128)} fusion(f32[128,16,256]{0,2,1:T(8,128)S(1)} %get-tuple-element.528, f32[128,1,256]{0,1,2:T(1,128)S(1)} %bitcast.277, f32[128,3,256]{0,1,2:T(4,128)S(1)} %slice_multiply_fusion.12, f32[128,5,256]{0,1,2:T(8,128)S(1)} %slice_multiply_fusion.13), kind=kOutput, calls=%fused_computation.25.clone.1 | convolution fusion | flops 58097664 | bytes 3424256 | tf_op jit(solution)/shard_map/while/body/eval_jaxpr/transpose(jvp(cka,lka->cla))/dot_general | solution.py:58
  291.9 4.8 %fusion.283 = f32[256,128,16]{1,2,0:T(8,128)} fusion(f32[9,16,256]{0,1,2:T(8,128)S(1)} %copy.337, f32[128,1,256]{0,1,2:T(1,128)S(1)} %bitcast.278, f32[128,3,256]{0,1,2:T(4,128)S(1)} %slice_multiply_fusion.12, f32[128,5,256]{0,1,2:T(8,128)S(1)} %slice_multiply_fusion.13), kind=kOutput, calls=%fused_computation.40.clone.1 | convolution fusion | flops 58097664 | bytes 3424256 | tf_op jit(solution)/shard_map/while/body/eval_jaxpr/transpose(jvp(cka,lka->cla))/dot_general | solution.py:58
  298.9 4.8 %fusion.284 = f32[64,16,256]{2,0,1:T(8,128)S(1)} fusion(f32[128,16,256]{0,2,1:T(8,128)} %bitcast.270, f32[256,128,16]{1,2,0:T(8,128)} %fusion.283, f32[16,256]{1,0:T(8,128)S(1)} %dynamic-slice_bitcast_fusion.5, f32[64,128]{1,0:T(8,128)S(1)} %copy-done.17), kind=kOutput, calls=%fused_computation.35.clone.1 | convolution fusion | flops 403701760 | bytes 5292032 | tf_op jit(solution)/shard_map/while/body/eval_jaxpr/transpose(jvp(hka,hc->cka))/dot_general | solution.py:55
  303.8 2.4 bitcast_multiply_fusion.12
  307.8 22.7 %scatter_custom_fusion.9 = f32[128,512]{0,1:T(8,128)S(1)} fusion(s32[4096]{0:T(1024)S(1)} %bitcast.284, f32[4096,128]{1,0:T(8,128)} %bitcast.274, f32[]{:T(128)} %constant.107.clone.38..sunk), kind=kCustom, calls=%fused_computation.131.clone.1 | custom fusion | flops 524288 | bytes 262656 | tf_op jit(solution)/shard_map/while/body/eval_jaxpr/transpose(jvp())/scatter-add | solution.py:127
  334.9 2.9 collective-permute-done.5
  339.8 4.3 fusion.293
  344.2 6.2 %fusion.288 = f32[256,9,16]{2,1,0:T(8,128)} fusion(f32[128,16,256]{0,2,1:T(8,128)S(1)} %copy-done.4, f32[128,1,256]{0,1,2:T(1,128)S(1)} %bitcast.276, f32[128,3,256]{0,1,2:T(4,128)S(1)} %slice_multiply_fusion.14, f32[128,5,256]{0,1,2:T(8,128)S(1)} %slice_multiply_fusion.15), kind=kOutput, calls=%fused_computation.29.clone.1 | convolution fusion | flops 58097664 | bytes 3424256 | tf_op jit(solution)/shard_map/while/body/eval_jaxpr/transpose(jvp(cka,lka->cla))/dot_general | solution.py:58
  350.4 2.3 copy.338
  353.5 3.6 fusion.294
  361.4 22.8 %scatter_fusion = f32[3,512]{0,1:T(8,128)S(1)} fusion(f32[3,512]{0,1:T(8,128)S(1)} %pad.328, s32[4096]{0:T(1024)S(1)} %bitcast.285, f32[4096,3]{1,0:T(8,128)} %bitcast.272), kind=kCustom, calls=%fused_computation.3.clone.1 | custom fusion | flops 12288 | bytes 163840 | tf_op jit(solution)/shard_map/while/body/eval_jaxpr/transpose(jvp())/scatter-add | solution.py:115
  384.2 22.5 %scatter_fusion.1 = f32[3,512]{0,1:T(8,128)S(1)} fusion(f32[3,512]{0,1:T(8,128)S(1)} %pad.329, s32[4096]{0:T(1024)S(1)} %bitcast.286, f32[4096,3]{1,0:T(8,128)S(1)} %bitcast.271), kind=kCustom, calls=%fused_computation.4.clone.1 | custom fusion | flops 12288 | bytes 163840 | tf_op jit(solution)/shard_map/while/body/eval_jaxpr/transpose(jvp())/scatter-add | solution.py:122
  411.1 2.8 collective-permute-done.7
  417.1 17.1 %all-reduce.19 = (f32[2]{0:T(128)S(1)}, f32[2]{0:T(128)S(1)}, f32[2]{0:T(128)S(1)}, f32[2]{0:T(128)S(1)}, f32[2]{0:T(128)S(1)}) all-reduce(f32[2]{0:T(128)S(1)} %get-tuple-element.388, f32[2]{0:T(128)S(1)} %get-tuple-element.308, f32[2]{0:T(128)S(1)} %get-tuple-element.307, ...), channel_id=1, replica_groups=mesh['image'=4,'space'=8] {'space'}, use_global_device_ids=true, to_apply=%region_21.22 | all-reduce | flops 10 | bytes 80 | tf_op jit(solution)/shard_map/psum | solution.py:172
  436.2 40.0 %all-reduce.18 = (f32[]{:T(128)}, f32[]{:T(128)}) all-reduce(f32[]{:T(128)} %multiply_reduce_fusion.14, f32[]{:T(128)} %get-tuple-element.354), channel_id=1, replica_groups=mesh['image'=4,'space'=8] {'image','space'}, use_global_device_ids=true, to_apply=%region_27.28 | all-reduce | flops 2 | bytes 16 | tf_op jit(solution)/shard_map/psum | solution.py:183
  (316 shorter events, 84.1 us)
Async XLA Ops:
  2.6 8.9 %copy-start.32 = (f32[1,3,256]{2,1,0:T(4,128)}, f32[1,3,256]{2,1,0:T(4,128)S(1)}, u32[]{:S(2)}) copy-start(f32[1,3,256]{2,1,0:T(4,128)S(1)} %get-tuple-element.391) | copy-start | bytes 9220
  2.6 8.9 %copy-start.33 = (f32[1,3,256]{2,1,0:T(4,128)}, f32[1,3,256]{2,1,0:T(4,128)S(1)}, u32[]{:S(2)}) copy-start(f32[1,3,256]{2,1,0:T(4,128)S(1)} %get-tuple-element.392) | copy-start | bytes 9220
  2.6 7.0 %collective-permute-start.9 = (f32[1,3,256]{2,1,0:T(4,128)S(1)}, f32[1,3,256]{2,1,0:T(4,128)S(1)}, u32[]{:S(2)}, u32[]{:S(2)}) collective-permute-start(f32[1,3,256]{2,1,0:T(4,128)S(1)} %get-tuple-element.391), channel_id=1, source_target_pairs={{0,8},{8,16},{16,24},{1,9},{9,17},{17,25},{2,10},{10,18},{18,26},{... | collective-permute-start | bytes 9224 | tf_op jit(solution)/shard_map/ppermute | solution.py:19
  5.0 5.9 %collective-permute-start.8 = (f32[1,3,256]{2,1,0:T(4,128)S(1)}, f32[1,3,256]{2,1,0:T(4,128)S(1)}, u32[]{:S(2)}, u32[]{:S(2)}) collective-permute-start(f32[1,3,256]{2,1,0:T(4,128)S(1)} %get-tuple-element.392), channel_id=1, source_target_pairs={{8,0},{16,8},{24,16},{9,1},{17,9},{25,17},{10,2},{18,10},{26,18},{... | collective-permute-start | bytes 9224 | tf_op jit(solution)/shard_map/ppermute | solution.py:21
  12.2 25.4 %copy-start.10 = (f32[3,256]{1,0:T(4,128)}, f32[3,256]{1,0:T(4,128)S(1)}, u32[]{:S(2)}) copy-start(f32[3,256]{1,0:T(4,128)S(1)} %dynamic-slice_bitcast_fusion.4) | copy-start | bytes 9220 | tf_op jit(solution)/shard_map/while
  12.2 6.9 %collective-permute-start = (f32[3,128]{1,0:T(4,128)S(1)}, f32[3,128]{1,0:T(4,128)S(1)}, u32[]{:S(2)}, u32[]{:S(2)}) collective-permute-start(f32[3,128]{1,0:T(4,128)S(1)} %get-tuple-element.520), channel_id=1, source_target_pairs={{1,0},{2,1},{3,2},{4,3},{5,4},{6,5},{7,6},{0,7},{9,8},{10,9},{11,1... | collective-permute-start | bytes 4616 | tf_op jit(solution)/shard_map/while/body/eval_jaxpr/ppermute | solution.py:21
  17.6 6.3 %collective-permute-start.1 = (f32[3,128]{1,0:T(4,128)S(1)}, f32[3,128]{1,0:T(4,128)S(1)}, u32[]{:S(2)}, u32[]{:S(2)}) collective-permute-start(f32[3,128]{1,0:T(4,128)S(1)} %get-tuple-element.521), channel_id=1, source_target_pairs={{0,1},{1,2},{2,3},{3,4},{4,5},{5,6},{6,7},{7,0},{8,9},{9,10},{10,1... | collective-permute-start | bytes 4616 | tf_op jit(solution)/shard_map/while/body/eval_jaxpr/ppermute | solution.py:19
  19.0 16.4 %copy-start.16 = (s32[4096]{0:T(1024)}, s32[4096]{0:T(1024)S(1)}, u32[]{:S(2)}) copy-start(s32[4096]{0:T(1024)S(1)} %broadcast_clamp_fusion.2) | copy-start | bytes 49156 | tf_op jit(solution)/shard_map/while
  19.0 18.5 %copy-start.26 = (f32[8]{0:T(128)}, f32[8]{0:T(128)S(1)}, u32[]{:S(2)}) copy-start(f32[8]{0:T(128)S(1)} %convert_multiply_fusion.2) | copy-start | bytes 100 | tf_op jit(solution)/shard_map/while
  47.1 6.6 %copy-start.1 = (f32[128,9,256]{0,1,2:T(8,128)}, f32[128,9,256]{0,1,2:T(8,128)S(1)}, u32[]{:S(2)}) copy-start(f32[128,9,256]{0,1,2:T(8,128)S(1)} %multiply_bitcast_fusion.7) | copy-start | bytes 3538948 | tf_op jit(solution)/shard_map/while
  47.1 5.5 %copy-start.24 = (f32[8,64]{1,0:T(8,128)S(1)}, f32[8,64]{1,0:T(8,128)}, u32[]{:S(2)}) copy-start(f32[8,64]{1,0:T(8,128)} %get-tuple-element.599) | copy-start | bytes 6148 | tf_op jit(solution)/shard_map/while
  47.1 5.5 %copy-start.27 = (f32[8]{0:T(128)S(1)}, f32[8]{0:T(128)}, u32[]{:S(2)}) copy-start(f32[8]{0:T(128)} %copy-done.26) | copy-start | bytes 100 | tf_op jit(solution)/shard_map/while
  50.5 4.3 collective-permute-start.2
  50.6 7.5 %collective-permute-start.3 = (f32[128,128]{0,1:T(8,128)S(1)}, f32[128,128]{0,1:T(8,128)S(1)}, u32[]{:S(2)}, u32[]{:S(2)}) collective-permute-start(f32[128,128]{0,1:T(8,128)S(1)} %get-tuple-element.527), channel_id=1, source_target_pairs={{0,1},{1,2},{2,3},{3,4},{4,5},{5,6},{6,7},{7,0},{8,9},{9,10},{10,1... | collective-permute-start | bytes 196616 | tf_op jit(solution)/shard_map/while/body/eval_jaxpr/ppermute | solution.py:19
  100.1 34.0 %copy-start.9 = (f32[256,9,16]{0,2,1:T(8,128)}, f32[256,9,16]{0,2,1:T(8,128)S(1)}, u32[]{:S(2)}) copy-start(f32[256,9,16]{0,2,1:T(8,128)S(1)} %copy.339) | copy-start | bytes 442372 | tf_op jit(solution)/shard_map/while
  100.1 4.8 %copy-start = (f32[256,128,16]{1,2,0:T(8,128)S(1)}, f32[256,128,16]{1,2,0:T(8,128)}, u32[]{:S(2)}) copy-start(f32[256,128,16]{1,2,0:T(8,128)} %fusion.283) | copy-start | bytes 6291460 | tf_op jit(solution)/shard_map/while
  100.1 4.8 %copy-start.5 = (f32[16,256,128]{2,1,0:T(8,128)S(1)}, f32[16,256,128]{2,1,0:T(8,128)}, u32[]{:S(2)}) copy-start(f32[16,256,128]{2,1,0:T(8,128)} %get-tuple-element.534) | copy-start | bytes 6291460 | tf_op jit(solution)/shard_map/while
  131.8 8.9 %copy-start.2 = (f32[128,9,256]{0,1,2:T(8,128)S(1)}, f32[128,9,256]{0,1,2:T(8,128)}, u32[]{:S(2)}) copy-start(f32[128,9,256]{0,1,2:T(8,128)} %copy-done.1) | copy-start | bytes 3538948 | tf_op jit(solution)/shard_map/while
  131.8 4.3 collective-permute-start.4
  131.9 7.2 %collective-permute-start.5 = (f32[128,128]{0,1:T(8,128)S(1)}, f32[128,128]{0,1:T(8,128)S(1)}, u32[]{:S(2)}, u32[]{:S(2)}) collective-permute-start(f32[128,128]{0,1:T(8,128)S(1)} %get-tuple-element.536), channel_id=1, source_target_pairs={{0,1},{1,2},{2,3},{3,4},{4,5},{5,6},{6,7},{7,0},{8,9},{9,10},{10,1... | collective-permute-start | bytes 196616 | tf_op jit(solution)/shard_map/while/body/eval_jaxpr/ppermute | solution.py:19
  153.9 4.7 copy-start.8
  153.9 4.7 copy-start.23
  153.9 4.7 copy-start.29
  162.2 49.3 %copy-start.36 = (f32[2]{0:T(128)S(1)}, f32[2]{0:T(128)}, u32[]{:S(2)}) copy-start(f32[2]{0:T(128)} %get-tuple-element.577) | copy-start | bytes 28 | tf_op jit(solution)/shard_map/while
  162.9 52.5 %copy-start.30 = (f32[2,3,256]{2,1,0:T(4,128)S(1)}, f32[2,3,256]{2,1,0:T(4,128)}, u32[]{:S(2)}) copy-start(f32[2,3,256]{2,1,0:T(4,128)} %get-tuple-element.576) | copy-start | bytes 18436 | tf_op jit(solution)/shard_map/while
  208.2 5.0 %collective-permute-start.6 = (f32[3,128]{0,1:T(8,128)S(1)}, f32[3,128]{0,1:T(8,128)S(1)}, u32[]{:S(2)}, u32[]{:S(2)}) collective-permute-start(f32[3,128]{0,1:T(8,128)S(1)} %get-tuple-element.555), channel_id=1, source_target_pairs={{1,0},{2,1},{3,2},{4,3},{5,4},{6,5},{7,6},{0,7},{9,8},{10,9},{11,1... | collective-permute-start | bytes 4616 | tf_op jit(solution)/shard_map/while/body/eval_jaxpr/ppermute | solution.py:21
  208.3 7.0 %collective-permute-start.7 = (f32[3,128]{0,1:T(8,128)S(1)}, f32[3,128]{0,1:T(8,128)S(1)}, u32[]{:S(2)}, u32[]{:S(2)}) collective-permute-start(f32[3,128]{0,1:T(8,128)S(1)} %get-tuple-element.556), channel_id=1, source_target_pairs={{0,1},{1,2},{2,3},{3,4},{4,5},{5,6},{6,7},{7,0},{8,9},{9,10},{10,1... | collective-permute-start | bytes 4616 | tf_op jit(solution)/shard_map/while/body/eval_jaxpr/ppermute | solution.py:19
  216.9 20.0 %copy-start.10 = (f32[3,256]{1,0:T(4,128)}, f32[3,256]{1,0:T(4,128)S(1)}, u32[]{:S(2)}) copy-start(f32[3,256]{1,0:T(4,128)S(1)} %dynamic-slice_bitcast_fusion.4) | copy-start | bytes 9220 | tf_op jit(solution)/shard_map/while
  216.9 3.6 collective-permute-start
  216.9 6.3 %collective-permute-start.1 = (f32[3,128]{1,0:T(4,128)S(1)}, f32[3,128]{1,0:T(4,128)S(1)}, u32[]{:S(2)}, u32[]{:S(2)}) collective-permute-start(f32[3,128]{1,0:T(4,128)S(1)} %get-tuple-element.521), channel_id=1, source_target_pairs={{0,1},{1,2},{2,3},{3,4},{4,5},{5,6},{6,7},{7,0},{8,9},{9,10},{10,1... | collective-permute-start | bytes 4616 | tf_op jit(solution)/shard_map/while/body/eval_jaxpr/ppermute | solution.py:19
  220.4 14.4 %copy-start.16 = (s32[4096]{0:T(1024)}, s32[4096]{0:T(1024)S(1)}, u32[]{:S(2)}) copy-start(s32[4096]{0:T(1024)S(1)} %broadcast_clamp_fusion.2) | copy-start | bytes 49156 | tf_op jit(solution)/shard_map/while
  220.4 16.5 %copy-start.26 = (f32[8]{0:T(128)}, f32[8]{0:T(128)S(1)}, u32[]{:S(2)}) copy-start(f32[8]{0:T(128)S(1)} %convert_multiply_fusion.2) | copy-start | bytes 100 | tf_op jit(solution)/shard_map/while
  246.4 6.2 %copy-start.1 = (f32[128,9,256]{0,1,2:T(8,128)}, f32[128,9,256]{0,1,2:T(8,128)S(1)}, u32[]{:S(2)}) copy-start(f32[128,9,256]{0,1,2:T(8,128)S(1)} %multiply_bitcast_fusion.7) | copy-start | bytes 3538948 | tf_op jit(solution)/shard_map/while
  246.5 5.2 %copy-start.24 = (f32[8,64]{1,0:T(8,128)S(1)}, f32[8,64]{1,0:T(8,128)}, u32[]{:S(2)}) copy-start(f32[8,64]{1,0:T(8,128)} %get-tuple-element.599) | copy-start | bytes 6148 | tf_op jit(solution)/shard_map/while
  246.5 5.2 %copy-start.27 = (f32[8]{0:T(128)S(1)}, f32[8]{0:T(128)}, u32[]{:S(2)}) copy-start(f32[8]{0:T(128)} %copy-done.26) | copy-start | bytes 100 | tf_op jit(solution)/shard_map/while
  249.5 4.3 collective-permute-start.2
  249.6 7.0 %collective-permute-start.3 = (f32[128,128]{0,1:T(8,128)S(1)}, f32[128,128]{0,1:T(8,128)S(1)}, u32[]{:S(2)}, u32[]{:S(2)}) collective-permute-start(f32[128,128]{0,1:T(8,128)S(1)} %get-tuple-element.527), channel_id=1, source_target_pairs={{0,1},{1,2},{2,3},{3,4},{4,5},{5,6},{6,7},{7,0},{8,9},{9,10},{10,1... | collective-permute-start | bytes 196616 | tf_op jit(solution)/shard_map/while/body/eval_jaxpr/ppermute | solution.py:19
  298.9 33.9 %copy-start.9 = (f32[256,9,16]{0,2,1:T(8,128)}, f32[256,9,16]{0,2,1:T(8,128)S(1)}, u32[]{:S(2)}) copy-start(f32[256,9,16]{0,2,1:T(8,128)S(1)} %copy.339) | copy-start | bytes 442372 | tf_op jit(solution)/shard_map/while
  298.9 4.8 %copy-start = (f32[256,128,16]{1,2,0:T(8,128)S(1)}, f32[256,128,16]{1,2,0:T(8,128)}, u32[]{:S(2)}) copy-start(f32[256,128,16]{1,2,0:T(8,128)} %fusion.283) | copy-start | bytes 6291460 | tf_op jit(solution)/shard_map/while
  298.9 4.8 %copy-start.5 = (f32[16,256,128]{2,1,0:T(8,128)S(1)}, f32[16,256,128]{2,1,0:T(8,128)}, u32[]{:S(2)}) copy-start(f32[16,256,128]{2,1,0:T(8,128)} %get-tuple-element.534) | copy-start | bytes 6291460 | tf_op jit(solution)/shard_map/while
  330.5 8.8 %copy-start.2 = (f32[128,9,256]{0,1,2:T(8,128)S(1)}, f32[128,9,256]{0,1,2:T(8,128)}, u32[]{:S(2)}) copy-start(f32[128,9,256]{0,1,2:T(8,128)} %copy-done.1) | copy-start | bytes 3538948 | tf_op jit(solution)/shard_map/while
  330.6 4.3 collective-permute-start.4
  330.6 7.2 %collective-permute-start.5 = (f32[128,128]{0,1:T(8,128)S(1)}, f32[128,128]{0,1:T(8,128)S(1)}, u32[]{:S(2)}, u32[]{:S(2)}) collective-permute-start(f32[128,128]{0,1:T(8,128)S(1)} %get-tuple-element.536), channel_id=1, source_target_pairs={{0,1},{1,2},{2,3},{3,4},{4,5},{5,6},{6,7},{7,0},{8,9},{9,10},{10,1... | collective-permute-start | bytes 196616 | tf_op jit(solution)/shard_map/while/body/eval_jaxpr/ppermute | solution.py:19
  352.6 4.5 copy-start.29
  360.8 49.3 %copy-start.36 = (f32[2]{0:T(128)S(1)}, f32[2]{0:T(128)}, u32[]{:S(2)}) copy-start(f32[2]{0:T(128)} %get-tuple-element.577) | copy-start | bytes 28 | tf_op jit(solution)/shard_map/while
  361.4 52.5 %copy-start.30 = (f32[2,3,256]{2,1,0:T(4,128)S(1)}, f32[2,3,256]{2,1,0:T(4,128)}, u32[]{:S(2)}) copy-start(f32[2,3,256]{2,1,0:T(4,128)} %get-tuple-element.576) | copy-start | bytes 18436 | tf_op jit(solution)/shard_map/while
  406.7 4.3 collective-permute-start.6
  406.8 7.0 %collective-permute-start.7 = (f32[3,128]{0,1:T(8,128)S(1)}, f32[3,128]{0,1:T(8,128)S(1)}, u32[]{:S(2)}, u32[]{:S(2)}) collective-permute-start(f32[3,128]{0,1:T(8,128)S(1)} %get-tuple-element.556), channel_id=1, source_target_pairs={{0,1},{1,2},{2,3},{3,4},{4,5},{5,6},{6,7},{7,0},{8,9},{9,10},{10,1... | collective-permute-start | bytes 4616 | tf_op jit(solution)/shard_map/while/body/eval_jaxpr/ppermute | solution.py:19
  (44 other events, 103.2 us)
where the time goes:
time: 484 us; the launch traced here: 480 us
  other arithmetic  158 us (33%)
  matrix products  118 us (24%)
  local copies, waits for them, and re-layouts  80.8 us (17%)
  blocking collectives  57.1 us (12%)
  waiting for transfers between devices  33.2 us (7%)
  starting transfers between devices  23.8 us (5%)
  loops' own time  5.98 us (1%)
    dot_general x12, matrix products, layer_out(): jnp.einsum('cka,lka->cla', radial, angular, precision=highest)  60.6 us
    scatter-add x2, other arithmetic, first_layer(): ext_pos[:, nb_idx]  45.6 us
    scatter-add x2, other arithmetic, second_energy(): ext_feat[:, nb_idx]  45.4 us
    scatter-add x2, other arithmetic, second_energy(): ext_pos[:, nb_idx]  45 us
    psum x1, blocking collectives, local(): lax.psum((jnp.sum(velocity * velocity), jnp.sum(neb_force * neb_force)),...  40 us
    dot_general x8, matrix products, layer_out(): jnp.einsum('hka,hc->cka', hidden, radial_b, precision=highest)  37.3 us
    gather x2, local copies, waits for them, and re-layouts, second_energy(): ext_feat[:, nb_idx]  30.9 us
    ppermute x9, waiting for transfers between devices, padded(): lax.ppermute(tail, axis, [(i, (i + 1) % count) for i in range(ends)])  24.3 us
  transfers between devices with their start and end apart: 18, of which 15 were waited for; matrix products, arithmetic and copies ran while one was open for 2% of the time, Pallas kernels for 0%

commit v1 on v0

v1 whole, which is shorter than its diff:
```python
import functools
import math

import jax
import jax.numpy as jnp
from jax import lax
from jax.experimental import pallas as pl
from jax.experimental.pallas import tpu as pltpu
from jax.sharding import PartitionSpec as P

f32 = jnp.float32
b16 = jnp.bfloat16
ROOT3 = math.sqrt(3.0)


def nn(a, b):
    return lax.dot_general(a, b, (((1,), (0,)), ((), ())), preferred_element_type=f32)


def nt(a, b):
    return lax.dot_general(a, b, (((1,), (1,)), ((), ())), preferred_element_type=f32)


def pieces(x):
    high = x.astype(b16).astype(f32)
    return high, x - high


def rows(*parts):
    return jnp.concatenate(parts, axis=0).astype(b16)


def eye(size):
    r = lax.broadcasted_iota(jnp.int32, (size, size), 0)
    c = lax.broadcasted_iota(jnp.int32, (size, size), 1)
    return jnp.where(r == c, 1.0, 0.0).astype(b16)


def total(x):
    return jnp.sum(jnp.sum(x, axis=1, keepdims=True), axis=0, keepdims=True)


def kernel(
    n_image,
    n_space,
    pos,
    vel,
    first_end,
    last_end,
    nbr,
    cnt,
    climb,
    a1,
    b1,
    m1,
    q1,
    a2,
    b2,
    m2,
    q2,
    neb_out,
    vel_out,
    pos_out,
    en_out,
    hot,
    ext,
    nbp,
    geo,
    ang,
    dang,
    dlen,
    rad1,
    rad2,
    feat_nb,
    slope1,
    slope2,
    mom1,
    mom2,
    oslope1,
    feat,
    gfeat,
    dq,
    drow,
    gpos,
    force,
    wa_f,
    wa_b1,
    wa_b2,
    wb_f1,
    wb_b1,
    wb_f2,
    wb_b2,
    wm_f1,
    wm_b1,
    wm_f2,
    wm_b2,
    rcol,
    energy,
    ghost_pos,
    ghost_feat,
    ghost_grad,
    ghost_force,
    side_img,
    part_a,
    part_b,
    send_edge,
    recv_edge,
    send_feat,
    recv_feat,
    send_grad,
    recv_grad,
    send_force,
    recv_force,
    send_a,
    recv_a,
    send_b,
    recv_b,
):
    imgs, _, atoms = pos.shape
    ghost = atoms // 2
    span = atoms + 2 * ghost
    slots = nbr.shape[1]
    hid = a1.shape[1]
    nb = a1.shape[0]
    ch = b1.shape[1]
    me_i = lax.axis_index("image")
    me_s = lax.axis_index("space")
    low = lax.rem(me_s + n_space - 1, n_space)
    upp = lax.rem(me_s + 1, n_space)
    prv = lax.rem(me_i + n_image - 1, n_image)
    nxt = lax.rem(me_i + 1, n_image)
    mesh_id = pl.DeviceIdType.MESH

    def remote(src, dst, ss, rs, dev):
        return pltpu.make_async_remote_copy(
            src_ref=src, dst_ref=dst, send_sem=ss, recv_sem=rs, device_id=dev, device_id_type=mesh_id
        )

    barrier = pltpu.get_barrier_semaphore()
    for off in range(1, n_space):
        pl.semaphore_signal(
            barrier, inc=1, device_id=(me_i, lax.rem(me_s + off, n_space)), device_id_type=mesh_id
        )
    for off in range(1, n_image):
        pl.semaphore_signal(
            barrier, inc=1, device_id=(lax.rem(me_i + off, n_image), me_s), device_id_type=mesh_id
        )

    place = lax.broadcasted_iota(jnp.int32, (span, atoms), 0)

    def lanes(k):
        return pl.ds(pl.multiple_of(k * atoms, atoms), atoms)

    for i in range(imgs):

        def build(k, carry, i=i):
            idx = nbr[i, pl.ds(k, 1), :]
            idx = jnp.where(cnt[i : i + 1, :] > k, idx, -1)
            hot[i, :, lanes(k)] = jnp.where(place == idx, 1.0, 0.0).astype(b16)
            return carry

        if i == 0:
            lax.fori_loop(0, slots, build, 0)
            pl.semaphore_wait(barrier, n_space - 1 + n_image - 1)
            edge = [
                remote(
                    pos.at[:, :, pl.ds(0, ghost)],
                    ghost_pos.at[1],
                    send_edge.at[0],
                    recv_edge.at[0],
                    (me_i, low),
                ),
                remote(
                    pos.at[:, :, pl.ds(atoms - ghost, ghost)],
                    ghost_pos.at[0],
                    send_edge.at[1],
                    recv_edge.at[1],
                    (me_i, upp),
                ),
                remote(
                    pos.at[0], side_img.at[1], send_edge.at[2], recv_edge.at[2], (prv, me_s)
                ),
                remote(
                    pos.at[imgs - 1], side_img.at[0], send_edge.at[3], recv_edge.at[3], (nxt, me_s)
                ),
            ]
            for c in edge:
                c.start()
        else:
            lax.fori_loop(0, slots, build, 0)

    fwd_a = []
    for a, wab in ((a1, wa_b1), (a2, wa_b2)):
        hi, lo = pieces(a[...])
        fwd_a.append(nt(eye(hid), rows(hi, hi, lo, lo)))
        both = jnp.concatenate([hi, lo], axis=0)
        wab[...] = jnp.concatenate([both, both], axis=1).astype(b16)
    wa_f[...] = rows(*fwd_a)
    unit = eye(ch)
    for b, wbf, wbb in ((b1, wb_f1, wb_b1), (b2, wb_f2, wb_b2)):
        hi, lo = pieces(b[...])
        wbf[...] = nt(unit, rows(hi, hi, lo)).astype(b16)
        both = jnp.concatenate([hi, lo], axis=0)
        wbb[...] = jnp.concatenate([both, both], axis=1).astype(b16)
    for m, wmf, wmb in ((m1, wm_f1, wm_b1), (m2, wm_f2, wm_b2)):
        hi, lo = pieces(m[...])
        wmf[...] = nt(unit, rows(hi, hi, lo)).astype(b16)
        both = jnp.concatenate([hi, lo], axis=0)
        wmb[...] = jnp.concatenate([both, both], axis=1).astype(b16)
    for j, q in enumerate((q1, q2)):
        wide = jnp.broadcast_to(q[...], (atoms, ch))
        hi, rest = pieces(wide)
        mid, lo = pieces(rest)
        rcol[j] = nt(unit, hi.astype(b16)) + nt(unit, mid.astype(b16)) + nt(unit, lo.astype(b16))

    centre = 0.5 * lax.broadcasted_iota(jnp.int32, (nb, atoms), 0).astype(f32)
    cstep = 32
    lt = 128

    def moments(i, rad, scale_by, mom):
        def block(cb, carry):
            cs = pl.ds(pl.multiple_of(cb * cstep, cstep), cstep)
            for t in range(atoms // lt):
                ls = pl.ds(t * lt, lt)
                acc = [None] * 9
                for k in range(slots):
                    r = rad[i, k, cs, ls]
                    if scale_by is not None:
                        r = r * scale_by[k, cs, ls]
                    for l in range(9):
                        term = r if l == 0 else r * ang[i, l, k : k + 1, ls]
                        acc[l] = term if k == 0 else acc[l] + term
                for l in range(9):
                    mom[l, cs, ls] = acc[l] * (1.0 / slots)
            return carry

        lax.fori_loop(0, ch // cstep, block, 0)

    def mixed(mom, wmf):
        inv0 = mom[0]
        inv1 = mom[1] * mom[1] + mom[2] * mom[2] + mom[3] * mom[3]
        inv2 = (
            mom[4] * mom[4]
            + mom[5] * mom[5]
            + mom[6] * mom[6]
            + mom[7] * mom[7]
            + mom[8] * mom[8]
        )
        h0, l0 = pieces(inv0)
        h1, l1 = pieces(inv1)
        h2, l2 = pieces(inv2)
        pre = nn(wmf[...], rows(h0, h1, h2, l0, l1, l2, h0, h1, h2))
        sig = 1.0 / (1.0 + jnp.exp(-pre))
        return pre * sig, sig * (1.0 + pre * (1.0 - sig))

    def unmixed(mom, wmb, dpre):
        hi, lo = pieces(dpre)
        both = nn(wmb[...], rows(hi, lo))
        dinv = (both[: 3 * ch] + both[3 * ch :]) * (1.0 / slots)
        mom[0] = dinv[:ch]
        d1 = 2.0 * dinv[ch : 2 * ch]
        d2 = 2.0 * dinv[2 * ch :]
        for l in range(1, 9):
            mom[l] = mom[l] * (d1 if l < 4 else d2)

    def radial_back(i, k, drad, wbb, wab, slope, add):
        hi, lo = pieces(drad)
        both = nn(wbb[...], rows(hi, lo))
        dz = (both[:hid] + both[hid:]) * slope[i, k]
        zh, zl = pieces(dz)
        db = nn(wab[...], rows(zh, zl))
        gap = geo[i, 3, pl.ds(k, 1), :] - centre
        dd = jnp.sum((db[:nb] + db[nb:]) * jnp.exp(-2.0 * gap * gap) * (-4.0 * gap), axis=0, keepdims=True)
        if add:
            dd = dd + dlen[i, pl.ds(k, 1), :]
        dlen[i, pl.ds(k, 1), :] = dd

    def phase_one(i):
        ext[...] = jnp.zeros_like(ext)
        ext[0:3, pl.ds(0, ghost)] = ghost_pos[0, i]
        ext[0:3, pl.ds(ghost, atoms)] = pos[i]
        ext[0:3, pl.ds(ghost + atoms, ghost)] = ghost_pos[1, i]
        hi, rest = pieces(ext[...])
        mid, lo = pieces(rest)
        three = rows(hi, mid, lo, jnp.zeros_like(lo))

        def pick(k, carry):
            got = nn(three, hot[i, :, lanes(k)])
            got = got[0:8] + got[8:16] + got[16:24]
            for c in range(3):
                nbp[c, pl.ds(k, 1), :] = got[c : c + 1]
            return carry

        lax.fori_loop(0, slots, pick, 0)
        r = [nbp[c] - pos[i, c : c + 1, :] for c in range(3)]
        sq = r[0] * r[0] + r[1] * r[1] + r[2] * r[2] + 1.0
        length = jnp.sqrt(sq)
        inverse = 1.0 / length
        ux, uy, uz = r[0] * inverse, r[1] * inverse, r[2] * inverse
        geo[i, 0], geo[i, 1], geo[i, 2], geo[i, 3] = ux, uy, uz, length
        ang[i, 1], ang[i, 2], ang[i, 3] = ux, uy, uz
        ang[i, 4] = ux * uy
        ang[i, 5] = uy * uz
        ang[i, 6] = ux * uz
        ang[i, 7] = 0.5 * (ux * ux - uy * uy)
        ang[i, 8] = (3.0 * uz * uz - 1.0) / (2.0 * ROOT3)

        def radial(k, carry):
            gap = geo[i, 3, pl.ds(k, 1), :] - centre
            hi, lo = pieces(jnp.exp(-2.0 * gap * gap))
            z = nn(wa_f[...], rows(hi, lo, hi, lo))
            sig = 1.0 / (1.0 + jnp.exp(-z))
            h = z * sig
            slope = sig * (1.0 + z * (1.0 - sig))
            slope1[i, k] = slope[:hid]
            slope2[i, k] = slope[hid:]
            hh, hl = pieces(h)
            alive = jnp.where(cnt[i : i + 1, :] > k, 1.0, 0.0)
            rad1[i, k] = nn(wb_f1[...], rows(hh[:hid], hl[:hid], hh[:hid])) * alive
            rad2[i, k] = nn(wb_f2[...], rows(hh[hid:], hl[hid:], hh[hid:]))
            return carry

        lax.fori_loop(0, slots, radial, 0)
        moments(i, rad1, None, mom1.at[i])
        out, slope = mixed(mom1.at[i], wm_f1)
        oslope1[i] = slope
        feat[i] = out
        energy[i] = total(out * rcol[0])

    def phase_two(i):
        whole = jnp.concatenate([ghost_feat[0, i], feat[i], ghost_feat[1, i]], axis=1)
        two = rows(*pieces(whole))

        def pick(k, carry):
            got = nn(two, hot[i, :, lanes(k)])
            feat_nb[k] = got[:ch] + got[ch:]
            return carry

        lax.fori_loop(0, slots, pick, 0)
        moments(i, rad2, feat_nb, mom2)
        out, slope = mixed(mom2, wm_f2)
        energy[i] = energy[i] + total(out * rcol[1])
        unmixed(mom2, wm_b2, rcol[1] * slope)

        def back(k, carry):
            row = [None] + [ang[i, l, pl.ds(k, 1), :] for l in range(1, 9)]
            sums = []
            for t in range(atoms // lt):
                ls = pl.ds(t * lt, lt)
                ys = [None] + [
                    jnp.broadcast_to(row[l][:, t * lt : (t + 1) * lt], (8, lt)) for l in range(1, 9)
                ]
                dy = [None] * 9
                for c in range(ch // 8):
                    cs = pl.ds(c * 8, 8)
                    raw = rad2[i, k, cs, ls]
                    q = feat_nb[k, cs, ls]
                    full = raw * q
                    drf = mom2[0, cs, ls]
                    for l in range(1, 9):
                        g = mom2[l, cs, ls]
                        drf = drf + g * ys[l]
                        dy[l] = g * full if c == 0 else dy[l] + g * full
                    rad2[i, k, cs, ls] = drf * q
                    feat_nb[k, cs, ls] = drf * raw
                sums.append([jnp.sum(dy[l], axis=0, keepdims=True) for l in range(1, 9)])
            for l in range(1, 9):
                dang[i, l, pl.ds(k, 1), :] = jnp.concatenate([s[l - 1] for s in sums], axis=1)
            dq[:, lanes(k)] = rows(*pieces(feat_nb[k]))
            radial_back(i, k, rad2[i, k], wb_b2, wa_b2, slope2, False)
            return carry

        lax.fori_loop(0, slots, back, 0)
        both = nt(dq[...], hot[i])
        gfeat[i] = both[:ch] + both[ch:]

    def phase_three(i):
        own = gfeat[i, :, pl.ds(ghost, atoms)]
        back_in = jnp.concatenate([ghost_grad[0, i], ghost_grad[1, i]], axis=1)
        unmixed(mom1.at[i], wm_b1, (own + back_in + rcol[0]) * oslope1[i])

        def back(k, carry):
            row = [None] + [ang[i, l, pl.ds(k, 1), :] for l in range(1, 9)]
            sums = []
            for t in range(atoms // lt):
                ls = pl.ds(t * lt, lt)
                ys = [None] + [
                    jnp.broadcast_to(row[l][:, t * lt : (t + 1) * lt], (8, lt)) for l in range(1, 9)
                ]
                alive = jnp.broadcast_to(jnp.where(cnt[i : i + 1, ls] > k, 1.0, 0.0), (8, lt))
                dy = [None] * 9
                for c in range(ch // 8):
                    cs = pl.ds(c * 8, 8)
                    full = rad1[i, k, cs, ls]
                    drf = mom1[i, 0, cs, ls]
                    for l in range(1, 9):
                        g = mom1[i, l, cs, ls]
                        drf = drf + g * ys[l]
                        dy[l] = g * full if c == 0 else dy[l] + g * full
                    rad1[i, k, cs, ls] = drf * alive
                sums.append([jnp.sum(dy[l], axis=0, keepdims=True) for l in range(1, 9)])
            for l in range(1, 9):
                dang[i, l, pl.ds(k, 1), :] = dang[i, l, pl.ds(k, 1), :] + jnp.concatenate(
                    [s[l - 1] for s in sums], axis=1
                )
            radial_back(i, k, rad1[i, k], wb_b1, wa_b1, slope1, True)
            return carry

        lax.fori_loop(0, slots, back, 0)
        ux, uy, uz, length = geo[i, 0], geo[i, 1], geo[i, 2], geo[i, 3]
        inverse = 1.0 / length
        y = [None] + [dang[i, l] for l in range(1, 9)]
        du = [
            y[1] + uy * y[4] + uz * y[6] + ux * y[7],
            y[2] + ux * y[4] + uz * y[5] - uy * y[7],
            y[3] + uy * y[5] + ux * y[6] + ROOT3 * uz * y[8],
        ]
        lean = dlen[i] - (du[0] * ux + du[1] * uy + du[2] * uz) * inverse
        drow[...] = jnp.zeros_like(drow)
        for c, u in enumerate((ux, uy, uz)):
            dr = du[c] * inverse + u * lean
            for k in range(slots):
                drow[c : c + 1, k * atoms : (k + 1) * atoms] = dr[k : k + 1]
            force[i, c : c + 1, :] = jnp.sum(dr, axis=0, keepdims=True)
        both = nt(rows(*pieces(drow[...])), hot[i])
        gpos[i] = both[:8] + both[8:]

    def swap(i, src, head, tail, dst_upper, dst_lower, ss, rs):
        pair = [
            remote(src.at[i, :, head], dst_upper.at[i], ss.at[i, 0], rs.at[i, 0], (me_i, low)),
            remote(src.at[i, :, tail], dst_lower.at[i], ss.at[i, 1], rs.at[i, 1], (me_i, upp)),
        ]
        for c in pair:
            c.start()
        return pair

    own_head, own_tail = pl.ds(0, ghost), pl.ds(atoms - ghost, ghost)
    ext_head, ext_tail = pl.ds(0, ghost), pl.ds(ghost + atoms, ghost)
    for c in edge:
        c.wait()
    sent = []
    for i in range(imgs):
        phase_one(i)
        sent.append(
            swap(
                i, feat, own_head, own_tail, ghost_feat.at[1], ghost_feat.at[0], send_feat, recv_feat
            )
        )
    back_sent = []
    for i in range(imgs):
        for c in sent[i]:
            c.wait()
        phase_two(i)
        back_sent.append(
            swap(
                i, gfeat, ext_head, ext_tail, ghost_grad.at[1], ghost_grad.at[0], send_grad, recv_grad
            )
        )
    force_sent = []
    for i in range(imgs):
        for c in back_sent[i]:
            c.wait()
        phase_three(i)
        force_sent.append(
            swap(
                i, gpos, ext_head, ext_tail, ghost_force.at[1], ghost_force.at[0], send_force, recv_force
            )
        )

    lane = lax.broadcasted_iota(jnp.int32, (8, 128), 1)
    line = lax.broadcasted_iota(jnp.int32, (8, 128), 0)
    spreads = []
    vv = jnp.zeros((1, 1), f32)
    block = jnp.zeros((8, 128), f32)
    for i in range(imgs):
        here = pos[i]
        if i == 0:
            before = jnp.where(me_i == 0, first_end[...], side_img[0])
        else:
            before = pos[i - 1]
        if i == imgs - 1:
            after = jnp.where(me_i == n_image - 1, last_end[...], side_img[1])
        else:
            after = pos[i + 1]
        spread = after - before
        spreads.append(spread)
        ahead = after - here
        behind = here - before
        vv = vv + total(vel[i] * vel[i])
        for c in force_sent[i]:
            c.wait()
        back_in = jnp.concatenate([ghost_force[0, i], ghost_force[1, i]], axis=1)
        f = force[i] - gpos[i, 0:3, pl.ds(ghost, atoms)] - back_in[0:3]
        force[i] = f
        values = (
            total(ahead * ahead),
            total(behind * behind),
            total(spread * spread),
            energy[i],
            total(f * spread),
            total(f * f),
        )
        for j, v in enumerate(values):
            block = jnp.where((line == i) & (lane == j), v, block)
    block = jnp.where((line == imgs) & (lane == 0), vv, block)

    def everywhere(block, part, ss, rs, count, mine, device):
        part[mine] = block
        out = []
        for off in range(1, count):
            peer = lax.rem(mine + off, count)
            c = remote(part.at[mine], part.at[mine], ss.at[off], rs.at[mine], device(peer))
            c.start()
            out.append(c)
        for off in range(1, count):
            peer = lax.rem(mine + off, count)
            remote(
                part.at[mine], part.at[peer], ss.at[off], rs.at[peer], device(peer)
            ).wait_recv()
        for c in out:
            c.wait_send()
        summed = part[0]
        for j in range(1, count):
            summed = summed + part[j]
        return summed

    summed = everywhere(block, part_a, send_a, recv_a, n_space, me_s, lambda p: (me_i, p))
    coefs = []
    ff = jnp.zeros((1, 1), f32)
    for i in range(imgs):
        sa, sb, st, en, fd, fs = [summed[i : i + 1, j : j + 1] for j in range(6)]
        norm = jnp.sqrt(st + 1e-06)
        along = fd / norm
        spring = 5.0 * (jnp.sqrt(sa) - jnp.sqrt(sb))
        climbing = jnp.where(me_i * imgs + i == climb[0], 1.0, 0.0)
        coef = (-(1.0 + climbing) * along + (1.0 - climbing) * spring) / norm
        coefs.append(coef)
        ff = ff + jnp.maximum(fs + 2.0 * coef * fd + coef * coef * st, 0.0)
        en_out[i : i + 1, :] = jnp.broadcast_to(en / (atoms * n_space), (1, 128))
    block = jnp.where(lane == 0, summed[imgs : imgs + 1, 0:1], 0.0)
    block = jnp.where(lane == 1, ff, block)
    summed = everywhere(block, part_b, send_b, recv_b, n_image, me_i, lambda p: (p, me_s))
    ratio = 0.1 * jnp.sqrt(summed[0:1, 0:1] / (summed[0:1, 1:2] + 1e-06)) + 0.1
    for i in range(imgs):
        neb = force[i] + coefs[i] * spreads[i]
        moved = 0.9 * vel[i] + ratio * neb
        neb_out[i] = neb
        vel_out[i] = moved
        pos_out[i] = pos[i] + 0.1 * moved


def local(n_image, n_space, *args):
    pos, nbr, a1, b1 = args[0], args[4], args[7], args[8]
    imgs, _, atoms = pos.shape
    slots = nbr.shape[1]
    nb, hid = a1.shape
    ch = b1.shape[1]
    ghost = atoms // 2
    span = atoms + 2 * ghost
    edges = slots * atoms
    args = list(args)
    for j in (10, 14):
        args[j] = args[j].reshape(1, -1)
    vm = pltpu.VMEM
    dma = pltpu.SemaphoreType.DMA
    scratch = [
        vm((imgs, span, edges), b16),
        vm((8, span), f32),
        vm((3, slots, atoms), f32),
        vm((imgs, 4, slots, atoms), f32),
        vm((imgs, 9, slots, atoms), f32),
        vm((imgs, 9, slots, atoms), f32),
        vm((imgs, slots, atoms), f32),
        vm((imgs, slots, ch, atoms), f32),
        vm((imgs, slots, ch, atoms), f32),
        vm((slots, ch, atoms), f32),
        vm((imgs, slots, hid, atoms), f32),
        vm((imgs, slots, hid, atoms), f32),
        vm((imgs, 9, ch, atoms), f32),
        vm((9, ch, atoms), f32),
        vm((imgs, ch, atoms), f32),
        vm((imgs, ch, atoms), f32),
        vm((imgs, ch, span), f32),
        vm((2 * ch, edges), b16),
        vm((8, edges), f32),
        vm((imgs, 8, span), f32),
        vm((imgs, 3, atoms), f32),
        vm((2 * hid, 4 * nb), b16),
        vm((2 * nb, 2 * hid), b16),
        vm((2 * nb, 2 * hid), b16),
        vm((ch, 3 * hid), b16),
        vm((2 * hid, 2 * ch), b16),
        vm((ch, 3 * hid), b16),
        vm((2 * hid, 2 * ch), b16),
        vm((ch, 9 * ch), b16),
        vm((6 * ch, 2 * ch), b16),
        vm((ch, 9 * ch), b16),
        vm((6 * ch, 2 * ch), b16),
        vm((2, ch, atoms), f32),
        vm((imgs, 1, 1), f32),
        vm((2, imgs, 3, ghost), f32),
        vm((2, imgs, ch, ghost), f32),
        vm((2, imgs, ch, ghost), f32),
        vm((2, imgs, 8, ghost), f32),
        vm((2, 3, atoms), f32),
        vm((n_space, 8, 128), f32),
        vm((n_image, 8, 128), f32),
        dma((4,)),
        dma((4,)),
        dma((imgs, 2)),
        dma((imgs, 2)),
        dma((imgs, 2)),
        dma((imgs, 2)),
        dma((imgs, 2)),
        dma((imgs, 2)),
        dma((n_space,)),
        dma((n_space,)),
        dma((n_image,)),
        dma((n_image,)),
    ]
    in_specs = [pl.BlockSpec(memory_space=pltpu.VMEM)] * len(args)
    in_specs[6] = pl.BlockSpec(memory_space=pltpu.SMEM)
    state = jax.ShapeDtypeStruct(pos.shape, f32)
    neb, vel, new, en = pl.pallas_call(
        functools.partial(kernel, n_image, n_space),
        out_shape=[state, state, state, jax.ShapeDtypeStruct((imgs, 128), f32)],
        in_specs=in_specs,
        out_specs=[pl.BlockSpec(memory_space=pltpu.VMEM)] * 4,
        scratch_shapes=scratch,
        compiler_params=pltpu.CompilerParams(
            collective_id=0, has_side_effects=True, vmem_limit_bytes=56 * 1024 * 1024
        ),
    )(*args)
    return neb, vel, new, en[:, 0]


def solution(mesh):
    state = P("image", None, "space")
    end = P(None, "space")
    in_specs = (state, state, end, end, state, P("image", "space")) + (P(),) * 9
    out_specs = (state, state, state, P("image"))
    body = functools.partial(local, mesh.shape["image"], mesh.shape["space"])
    return jax.shard_map(body, mesh=mesh, in_specs=in_specs, out_specs=out_specs, check_vma=False)
```

time: 484 us -> 98.7 us (0.20)
  other arithmetic: 158 us -> 0 us
  matrix products: 118 us -> 0 us
  Pallas kernels: 0 us -> 92.1 us
  local copies, waits for them, and re-layouts: 80.8 us -> 5.02 us
  blocking collectives: 57.1 us -> 0 us
  waiting for transfers between devices: 33.2 us -> 0 us
  starting transfers between devices: 23.8 us -> 0 us
  loops' own time: 5.98 us -> 0 us
    scatter-add x6 -> x0, other arithmetic: 136 us -> none  [the longest x2 45.6 us: first_layer(): ext_pos[:, nb_idx]]
    dot_general x36 -> x0, matrix products: 118 us -> none  [the longest x12 60.6 us: layer_out(): jnp.einsum('cka,lka->cla', radial, angular, precision=highest)]
    pallas_call x0 -> x1, Pallas kernels: none -> 92.1 us  [local(): pl.pallas_call(functools.partial(kernel, n_image, n_space), out_shape=[st...]
    psum x2 -> x0, blocking collectives: 57.1 us -> none  [the longest x1 40 us: local(): lax.psum((jnp.sum(velocity * velocity), jnp.sum(neb_force * neb_force)),...]
    gather x6 -> x0, local copies, waits for them, and re-layouts: 53.6 us -> none  [the longest x2 30.9 us: second_energy(): ext_feat[:, nb_idx]]
    ppermute x18 -> x0, waiting for transfers between devices: 33.2 us -> none  [the longest x9 24.3 us: padded(): lax.ppermute(tail, axis, [(i, (i + 1) % count) for i in range(ends)])]
    ppermute x18 -> x0, starting transfers between devices: 23.8 us -> none  [the longest x9 16.8 us: padded(): lax.ppermute(tail, axis, [(i, (i + 1) % count) for i in range(ends)])]
    dot_general x4 -> x0, local copies, waits for them, and re-layouts: 8.79 us -> none  [layer_out(): jnp.einsum('cka,lka->cla', radial, angular, precision=highest)]
  transfers between devices with their start and end apart: 18 -> 0, of which waited for: 15 -> 0; matrix products, arithmetic and copies ran while one was open for 2% -> 0% of each run, Pallas kernels for 0% -> 0%
where the time goes in v1:
time: 98.7 us; the launch traced here: 98.5 us
  Pallas kernels  92.1 us (93%)
  local copies, waits for them, and re-layouts  5.02 us (5%)
  between operations  1.31 us (1%)
    pallas_call x1, Pallas kernels, local(): pl.pallas_call(functools.partial(kernel, n_image, n_space), out_shape=[st...  92.1 us
    unnamed x13, local copies, waits for them, and re-layouts  4.4 us

profile of v1, /device:TPU:0, one launch (start us, length us, event | category | flops | bytes accessed | tf_op | source)
XLA Modules:
  0.0 98.5 jit_solution(2901110509228597546)
XLA Ops:
  1.3 0.0 copy-start.2
  1.3 1.3 %copy.24.pos = f32[2,3,256]{2,1,0:T(4,128)} copy(f32[2,3,256]{2,0,1:T(2,128)} %param.15) | data formatting | bytes 12288 | tf_op args[0]
  2.6 0.0 copy-done.2
  2.6 0.6 copy.25.vel
  3.2 92.1 %shard_map.174 = (f32[2,3,256]{2,1,0:T(4,128)}, f32[2,3,256]{2,1,0:T(4,128)}, f32[2,3,256]{2,1,0:T(4,128)}, f32[2,128]{1,0:T(2,128)}) custom-call(f32[2,3,256]{2,1,0:T(4,128)} %copy.24.pos, f32[2,3,256]{2,1,0:T(4,128)} %copy.25.vel, f32[3,256]{1,0:T(4,128)} %first_end.1, f32[3,256]{1,0:T(4,128)} %last_end.1, s32[2,16,256]{2,1,0:T(8,128)} %nbr.1, ...), custom_call_target="tpu_custom_call" | custom-call | tf_op jit(solution)/shard_map/pallas_call | solution.py:624
  95.3 0.0 copy-start.3
  95.3 0.0 copy-start.1
  95.3 1.3 %copy.26 = f32[2,3,256]{2,0,1:T(2,128)} copy(f32[2,3,256]{2,1,0:T(4,128)} %get-tuple-element.16) | data formatting | bytes 12288
  96.6 0.0 copy-done.3
  96.6 0.0 copy-start
  96.6 0.6 slice_reduce_fusion
  97.3 0.0 copy-done.1
  97.3 0.6 copy.27
  97.9 0.0 copy-done
  97.9 0.6 copy.28
Async XLA Ops:
  1.3 1.3 %copy-start.2 = (f32[2,3,256]{2,0,1:T(2,128)S(1)}, f32[2,3,256]{2,0,1:T(2,128)}, u32[]{:S(2)}) copy-start(f32[2,3,256]{2,0,1:T(2,128)} %param.16) | copy-start | bytes 18436
  95.3 1.3 %copy-start.3 = (f32[2,128]{1,0:T(2,128)S(1)}, f32[2,128]{1,0:T(2,128)}, u32[]{:S(2)}) copy-start(f32[2,128]{1,0:T(2,128)} %get-tuple-element.11) | copy-start | bytes 3076
  95.3 1.9 %copy-start.1 = (f32[2,3,256]{2,1,0:T(4,128)S(1)}, f32[2,3,256]{2,1,0:T(4,128)}, u32[]{:S(2)}) copy-start(f32[2,3,256]{2,1,0:T(4,128)} %get-tuple-element.17) | copy-start | bytes 18436
  96.6 1.2 %copy-start = (f32[2,3,256]{2,1,0:T(4,128)S(1)}, f32[2,3,256]{2,1,0:T(4,128)}, u32[]{:S(2)}) copy-start(f32[2,3,256]{2,1,0:T(4,128)} %get-tuple-element.18) | copy-start | bytes 18436

commit v2 on v1

--- a/solution.py
+++ b/solution.py
@@ -43,8 +43,8 @@
 def kernel(
     n_image,
     n_space,
-    pos,
-    vel,
+    pos_in,
+    vel_in,
     first_end,
     last_end,
     nbr,
@@ -62,6 +62,8 @@
     vel_out,
     pos_out,
     en_out,
+    pos,
+    vel,
     hot,
     ext,
     nbp,
@@ -116,7 +118,7 @@
     send_b,
     recv_b,
 ):
-    imgs, _, atoms = pos.shape
+    _, imgs, atoms = pos_in.shape
     ghost = atoms // 2
     span = atoms + 2 * ghost
     slots = nbr.shape[1]
@@ -145,6 +147,11 @@
         pl.semaphore_signal(
             barrier, inc=1, device_id=(lax.rem(me_i + off, n_image), me_s), device_id_type=mesh_id
         )
+
+    for i in range(imgs):
+        for c in range(3):
+            pos[i, c : c + 1, :] = pos_in[c, i : i + 1, :]
+            vel[i, c : c + 1, :] = vel_in[c, i : i + 1, :]
 
     place = lax.broadcasted_iota(jnp.int32, (span, atoms), 0)
 
@@ -213,7 +220,13 @@
         mid, lo = pieces(rest)
         rcol[j] = nt(unit, hi.astype(b16)) + nt(unit, mid.astype(b16)) + nt(unit, lo.astype(b16))
 
-    centre = 0.5 * lax.broadcasted_iota(jnp.int32, (nb, atoms), 0).astype(f32)
+    group = 4 if slots % 4 == 0 else 1
+    pair = 2 if slots % 2 == 0 else 1
+    centre = 0.5 * lax.broadcasted_iota(jnp.int32, (nb, group * atoms), 0).astype(f32)
+
+    def wide(parts):
+        return jnp.concatenate(parts, axis=1)
+
     cstep = 32
     lt = 128
 
@@ -263,17 +276,24 @@
         for l in range(1, 9):
             mom[l] = mom[l] * (d1 if l < 4 else d2)
 
-    def radial_back(i, k, drad, wbb, wab, slope, add):
-        hi, lo = pieces(drad)
-        both = nn(wbb[...], rows(hi, lo))
-        dz = (both[:hid] + both[hid:]) * slope[i, k]
-        zh, zl = pieces(dz)
-        db = nn(wab[...], rows(zh, zl))
-        gap = geo[i, 3, pl.ds(k, 1), :] - centre
-        dd = jnp.sum((db[:nb] + db[nb:]) * jnp.exp(-2.0 * gap * gap) * (-4.0 * gap), axis=0, keepdims=True)
-        if add:
-            dd = dd + dlen[i, pl.ds(k, 1), :]
-        dlen[i, pl.ds(k, 1), :] = dd
+    def radial_back(i, drad, wbb, wab, slope, add):
+        def step(s, carry):
+            ks = [s * group + j for j in range(group)]
+            hi, lo = pieces(wide([drad[i, k] for k in ks]))
+            both = nn(wbb[...], rows(hi, lo))
+            dz = (both[:hid] + both[hid:]) * wide([slope[i, k] for k in ks])
+            zh, zl = pieces(dz)
+            db = nn(wab[...], rows(zh, zl))
+            gap = wide([geo[i, 3, pl.ds(k, 1), :] for k in ks]) - centre
+            db = (db[:nb] + db[nb:]) * jnp.exp(-2.0 * gap * gap) * (-4.0 * gap)
+            dd = jnp.sum(db, axis=0, keepdims=True)
+            if add:
+                dd = dd + wide([dlen[i, pl.ds(k, 1), :] for k in ks])
+            for j, k in enumerate(ks):
+                dlen[i, pl.ds(k, 1), :] = dd[:, j * atoms : (j + 1) * atoms]
+            return carry
+
+        lax.fori_loop(0, slots // group, step, 0)
 
     def phase_one(i):
         ext[...] = jnp.zeros_like(ext)
@@ -284,14 +304,11 @@
         mid, lo = pieces(rest)
         three = rows(hi, mid, lo, jnp.zeros_like(lo))
 
-        def pick(k, carry):
-            got = nn(three, hot[i, :, lanes(k)])
-            got = got[0:8] + got[8:16] + got[16:24]
+        got = nn(three, hot[i])
+        got = got[0:8] + got[8:16] + got[16:24]
+        for k in range(slots):
             for c in range(3):
-                nbp[c, pl.ds(k, 1), :] = got[c : c + 1]
-            return carry
-
-        lax.fori_loop(0, slots, pick, 0)
+                nbp[c, k : k + 1, :] = got[c : c + 1, k * atoms : (k + 1) * atoms]
         r = [nbp[c] - pos[i, c : c + 1, :] for c in range(3)]
         sq = r[0] * r[0] + r[1] * r[1] + r[2] * r[2] + 1.0
         length = jnp.sqrt(sq)
@@ -305,22 +322,27 @@
         ang[i, 7] = 0.5 * (ux * ux - uy * uy)
         ang[i, 8] = (3.0 * uz * uz - 1.0) / (2.0 * ROOT3)
 
-        def radial(k, carry):
-            gap = geo[i, 3, pl.ds(k, 1), :] - centre
+        def radial(s, carry):
+            ks = [s * group + j for j in range(group)]
+            gap = wide([geo[i, 3, pl.ds(k, 1), :] for k in ks]) - centre
             hi, lo = pieces(jnp.exp(-2.0 * gap * gap))
             z = nn(wa_f[...], rows(hi, lo, hi, lo))
             sig = 1.0 / (1.0 + jnp.exp(-z))
             h = z * sig
             slope = sig * (1.0 + z * (1.0 - sig))
-            slope1[i, k] = slope[:hid]
-            slope2[i, k] = slope[hid:]
             hh, hl = pieces(h)
-            alive = jnp.where(cnt[i : i + 1, :] > k, 1.0, 0.0)
-            rad1[i, k] = nn(wb_f1[...], rows(hh[:hid], hl[:hid], hh[:hid])) * alive
-            rad2[i, k] = nn(wb_f2[...], rows(hh[hid:], hl[hid:], hh[hid:]))
+            alive = wide([jnp.where(cnt[i : i + 1, :] > k, 1.0, 0.0) for k in ks])
+            r1 = nn(wb_f1[...], rows(hh[:hid], hl[:hid], hh[:hid])) * alive
+            r2 = nn(wb_f2[...], rows(hh[hid:], hl[hid:], hh[hid:]))
+            for j, k in enumerate(ks):
+                at = slice(j * atoms, (j + 1) * atoms)
+                slope1[i, k] = slope[:hid, at]
+                slope2[i, k] = slope[hid:, at]
+                rad1[i, k] = r1[:, at]
+                rad2[i, k] = r2[:, at]
             return carry
 
-        lax.fori_loop(0, slots, radial, 0)
+        lax.fori_loop(0, slots // group, radial, 0)
         moments(i, rad1, None, mom1.at[i])
         out, slope = mixed(mom1.at[i], wm_f1)
         oslope1[i] = slope
@@ -331,82 +353,102 @@
         whole = jnp.concatenate([ghost_feat[0, i], feat[i], ghost_feat[1, i]], axis=1)
         two = rows(*pieces(whole))
 
-        def pick(k, carry):
-            got = nn(two, hot[i, :, lanes(k)])
-            feat_nb[k] = got[:ch] + got[ch:]
+        def pick(s, carry):
+            cols = pl.ds(pl.multiple_of(s * group * atoms, group * atoms), group * atoms)
+            got = nn(two, hot[i, :, cols])
+            got = got[:ch] + got[ch:]
+            for j in range(group):
+                feat_nb[s * group + j] = got[:, j * atoms : (j + 1) * atoms]
             return carry
 
-        lax.fori_loop(0, slots, pick, 0)
+        lax.fori_loop(0, slots // group, pick, 0)
         moments(i, rad2, feat_nb, mom2)
         out, slope = mixed(mom2, wm_f2)
         energy[i] = energy[i] + total(out * rcol[1])
         unmixed(mom2, wm_b2, rcol[1] * slope)
 
-        def back(k, carry):
-            row = [None] + [ang[i, l, pl.ds(k, 1), :] for l in range(1, 9)]
-            sums = []
+        def back(s, carry):
+            ks = [s * pair + j for j in range(pair)]
+            row = [[None] + [ang[i, l, pl.ds(k, 1), :] for l in range(1, 9)] for k in ks]
+            sums = [[] for k in ks]
             for t in range(atoms // lt):
                 ls = pl.ds(t * lt, lt)
-                ys = [None] + [
-                    jnp.broadcast_to(row[l][:, t * lt : (t + 1) * lt], (8, lt)) for l in range(1, 9)
+                ys = [
+                    [None] + [jnp.broadcast_to(r[:, t * lt : (t + 1) * lt], (8, lt)) for r in w[1:]]
+                    for w in row
                 ]
-                dy = [None] * 9
+                dy = [[None] * 9 for k in ks]
                 for c in range(ch // 8):
                     cs = pl.ds(c * 8, 8)
-                    raw = rad2[i, k, cs, ls]
-                    q = feat_nb[k, cs, ls]
-                    full = raw * q
-                    drf = mom2[0, cs, ls]
+                    raw = [rad2[i, k, cs, ls] for k in ks]
+                    q = [feat_nb[k, cs, ls] for k in ks]
+                    full = [x * y for x, y in zip(raw, q)]
+                    drf = [mom2[0, cs, ls]] * pair
                     for l in range(1, 9):
                         g = mom2[l, cs, ls]
-                        drf = drf + g * ys[l]
-                        dy[l] = g * full if c == 0 else dy[l] + g * full
-                    rad2[i, k, cs, ls] = drf * q
-                    feat_nb[k, cs, ls] = drf * raw
-                sums.append([jnp.sum(dy[l], axis=0, keepdims=True) for l in range(1, 9)])
-            for l in range(1, 9):
-                dang[i, l, pl.ds(k, 1), :] = jnp.concatenate([s[l - 1] for s in sums], axis=1)
-            dq[:, lanes(k)] = rows(*pieces(feat_nb[k]))
-            radial_back(i, k, rad2[i, k], wb_b2, wa_b2, slope2, False)
+                        for j in range(pair):
+                            drf[j] = drf[j] + g * ys[j][l]
+                            term = g * full[j]
+                            dy[j][l] = term if c == 0 else dy[j][l] + term
+                    for j, k in enumerate(ks):
+                        rad2[i, k, cs, ls] = drf[j] * q[j]
+                        feat_nb[k, cs, ls] = drf[j] * raw[j]
+                for j in range(pair):
+                    sums[j].append([jnp.sum(x, axis=0, keepdims=True) for x in dy[j][1:]])
+            for j, k in enumerate(ks):
+                for l in range(1, 9):
+                    dang[i, l, pl.ds(k, 1), :] = wide([x[l - 1] for x in sums[j]])
+                dq[:, lanes(k)] = rows(*pieces(feat_nb[k]))
             return carry
 
-        lax.fori_loop(0, slots, back, 0)
+        lax.fori_loop(0, slots // pair, back, 0)
         both = nt(dq[...], hot[i])
         gfeat[i] = both[:ch] + both[ch:]
+
+    def phase_two_rest(i):
+        radial_back(i, rad2, wb_b2, wa_b2, slope2, False)
 
     def phase_three(i):
         own = gfeat[i, :, pl.ds(ghost, atoms)]
         back_in = jnp.concatenate([ghost_grad[0, i], ghost_grad[1, i]], axis=1)
         unmixed(mom1.at[i], wm_b1, (own + back_in + rcol[0]) * oslope1[i])
 
-        def back(k, carry):
-            row = [None] + [ang[i, l, pl.ds(k, 1), :] for l in range(1, 9)]
-            sums = []
+        def back(s, carry):
+            ks = [s * pair + j for j in range(pair)]
+            row = [[None] + [ang[i, l, pl.ds(k, 1), :] for l in range(1, 9)] for k in ks]
+            old = [[None] + [dang[i, l, pl.ds(k, 1), :] for l in range(1, 9)] for k in ks]
+            sums = [[] for k in ks]
             for t in range(atoms // lt):
                 ls = pl.ds(t * lt, lt)
-                ys = [None] + [
-                    jnp.broadcast_to(row[l][:, t * lt : (t + 1) * lt], (8, lt)) for l in range(1, 9)
+                ys = [
+                    [None] + [jnp.broadcast_to(r[:, t * lt : (t + 1) * lt], (8, lt)) for r in w[1:]]
+                    for w in row
                 ]
-                alive = jnp.broadcast_to(jnp.where(cnt[i : i + 1, ls] > k, 1.0, 0.0), (8, lt))
-                dy = [None] * 9
+                alive = [
+                    jnp.broadcast_to(jnp.where(cnt[i : i + 1, ls] > k, 1.0, 0.0), (8, lt)) for k in ks
+                ]
+                dy = [[None] * 9 for k in ks]
                 for c in range(ch // 8):
                     cs = pl.ds(c * 8, 8)
-                    full = rad1[i, k, cs, ls]
-                    drf = mom1[i, 0, cs, ls]
+                    full = [rad1[i, k, cs, ls] for k in ks]
+                    drf = [mom1[i, 0, cs, ls]] * pair
                     for l in range(1, 9):
                         g = mom1[i, l, cs, ls]
-                        drf = drf + g * ys[l]
-                        dy[l] = g * full if c == 0 else dy[l] + g * full
-                    rad1[i, k, cs, ls] = drf * alive
-                sums.append([jnp.sum(dy[l], axis=0, keepdims=True) for l in range(1, 9)])
-            for l in range(1, 9):
-                dang[i, l, pl.ds(k, 1), :] = dang[i, l, pl.ds(k, 1), :] + jnp.concatenate(
-                    [s[l - 1] for s in sums], axis=1
-                )
-            radial_back(i, k, rad1[i, k], wb_b1, wa_b1, slope1, True)
+                        for j in range(pair):
+                            drf[j] = drf[j] + g * ys[j][l]
+                            term = g * full[j]
+                            dy[j][l] = term if c == 0 else dy[j][l] + term
+                    for j, k in enumerate(ks):
+                        rad1[i, k, cs, ls] = drf[j] * alive[j]
+                for j in range(pair):
+                    sums[j].append([jnp.sum(x, axis=0, keepdims=True) for x in dy[j][1:]])
+            for j, k in enumerate(ks):
+                for l in range(1, 9):
+                    dang[i, l, pl.ds(k, 1), :] = old[j][l] + wide([x[l - 1] for x in sums[j]])
             return carry
 
-        lax.fori_loop(0, slots, back, 0)
+        lax.fori_loop(0, slots // pair, back, 0)
+        radial_back(i, rad1, wb_b1, wa_b1, slope1, True)
         ux, uy, uz, length = geo[i, 0], geo[i, 1], geo[i, 2], geo[i, 3]
         inverse = 1.0 / length
         y = [None] + [dang[i, l] for l in range(1, 9)]
@@ -426,13 +468,13 @@
         gpos[i] = both[:8] + both[8:]
 
     def swap(i, src, head, tail, dst_upper, dst_lower, ss, rs):
-        pair = [
+        both = [
             remote(src.at[i, :, head], dst_upper.at[i], ss.at[i, 0], rs.at[i, 0], (me_i, low)),
             remote(src.at[i, :, tail], dst_lower.at[i], ss.at[i, 1], rs.at[i, 1], (me_i, upp)),
         ]
-        for c in pair:
+        for c in both:
             c.start()
-        return pair
+        return both
 
     own_head, own_tail = pl.ds(0, ghost), pl.ds(atoms - ghost, ghost)
     ext_head, ext_tail = pl.ds(0, ghost), pl.ds(ghost + atoms, ghost)
@@ -456,6 +498,7 @@
                 i, gfeat, ext_head, ext_tail, ghost_grad.at[1], ghost_grad.at[0], send_grad, recv_grad
             )
         )
+        phase_two_rest(i)
     force_sent = []
     for i in range(imgs):
         for c in back_sent[i]:
@@ -528,7 +571,7 @@
     coefs = []
     ff = jnp.zeros((1, 1), f32)
     for i in range(imgs):
-        sa, sb, st, en, fd, fs = [summed[i : i + 1, j : j + 1] for j in range(6)]
+        sa, sb, st, fd, fs = [summed[i : i + 1, j : j + 1] for j in (0, 1, 2, 4, 5)]
         norm = jnp.sqrt(st + 1e-06)
         along = fd / norm
         spring = 5.0 * (jnp.sqrt(sa) - jnp.sqrt(sb))
@@ -536,7 +579,8 @@
         coef = (-(1.0 + climbing) * along + (1.0 - climbing) * spring) / norm
         coefs.append(coef)
         ff = ff + jnp.maximum(fs + 2.0 * coef * fd + coef * coef * st, 0.0)
-        en_out[i : i + 1, :] = jnp.broadcast_to(en / (atoms * n_space), (1, 128))
+        mine = jnp.where((line == i) & (lane == 3), summed, 0.0)
+        en_out[i] = jnp.sum(mine) * (1.0 / (atoms * n_space))
     block = jnp.where(lane == 0, summed[imgs : imgs + 1, 0:1], 0.0)
     block = jnp.where(lane == 1, ff, block)
     summed = everywhere(block, part_b, send_b, recv_b, n_image, me_i, lambda p: (p, me_s))
@@ -544,9 +588,11 @@
     for i in range(imgs):
         neb = force[i] + coefs[i] * spreads[i]
         moved = 0.9 * vel[i] + ratio * neb
-        neb_out[i] = neb
-        vel_out[i] = moved
-        pos_out[i] = pos[i] + 0.1 * moved
+        new = pos[i] + 0.1 * moved
+        for c in range(3):
+            neb_out[c, i : i + 1, :] = neb[c : c + 1]
+            vel_out[c, i : i + 1, :] = moved[c : c + 1]
+            pos_out[c, i : i + 1, :] = new[c : c + 1]
 
 
 def local(n_image, n_space, *args):
@@ -559,11 +605,15 @@
     span = atoms + 2 * ghost
     edges = slots * atoms
     args = list(args)
+    for j in (0, 1):
+        args[j] = jnp.transpose(args[j], (1, 0, 2))
     for j in (10, 14):
         args[j] = args[j].reshape(1, -1)
     vm = pltpu.VMEM
     dma = pltpu.SemaphoreType.DMA
     scratch = [
+        vm((imgs, 3, atoms), f32),
+        vm((imgs, 3, atoms), f32),
         vm((imgs, span, edges), b16),
         vm((8, span), f32),
         vm((3, slots, atoms), f32),
@@ -620,18 +670,20 @@
     ]
     in_specs = [pl.BlockSpec(memory_space=pltpu.VMEM)] * len(args)
     in_specs[6] = pl.BlockSpec(memory_space=pltpu.SMEM)
-    state = jax.ShapeDtypeStruct(pos.shape, f32)
+    state = jax.ShapeDtypeStruct((3, imgs, atoms), f32)
     neb, vel, new, en = pl.pallas_call(
         functools.partial(kernel, n_image, n_space),
-        out_shape=[state, state, state, jax.ShapeDtypeStruct((imgs, 128), f32)],
+        out_shape=[state, state, state, jax.ShapeDtypeStruct((imgs,), f32)],
         in_specs=in_specs,
-        out_specs=[pl.BlockSpec(memory_space=pltpu.VMEM)] * 4,
+        out_specs=[pl.BlockSpec(memory_space=pltpu.VMEM)] * 3
+        + [pl.BlockSpec(memory_space=pltpu.SMEM)],
         scratch_shapes=scratch,
         compiler_params=pltpu.CompilerParams(
             collective_id=0, has_side_effects=True, vmem_limit_bytes=56 * 1024 * 1024
         ),
     )(*args)
-    return neb, vel, new, en[:, 0]
+    neb, vel, new = [jnp.transpose(x, (1, 0, 2)) for x in (neb, vel, new)]
+    return neb, vel, new, en
 
 
 def solution(mesh):

time: 98.7 us -> 69.9 us (0.71)
  Pallas kernels: 92.1 us -> 65.1 us
  local copies, waits for them, and re-layouts: 5.02 us -> 3.18 us
    pallas_call x1, Pallas kernels: 92.1 us -> 65.1 us  [local(): pl.pallas_call(functools.partial(kernel, n_image, n_space), out_shape=[st...]
    unnamed x13 -> x12, local copies, waits for them, and re-layouts: 4.4 us -> 3.18 us
where the time goes in v2:
time: 69.9 us; the launch traced here: 69.6 us
  Pallas kernels  65.1 us (93%)
  local copies, waits for them, and re-layouts  3.18 us (5%)
  between operations  1.3 us (2%)
    pallas_call x1, Pallas kernels, local(): pl.pallas_call(functools.partial(kernel, n_image, n_space), out_shape=[st...  65.1 us
    unnamed x12, local copies, waits for them, and re-layouts  3.18 us

profile of v2, /device:TPU:0, one launch (start us, length us, event | category | flops | bytes accessed | tf_op | source)
XLA Modules:
  0.0 69.6 jit_solution(15402685523689664574)
XLA Ops:
  1.3 65.1 %shard_map.174 = (f32[3,2,256]{2,1,0:T(2,128)}, f32[3,2,256]{2,1,0:T(2,128)}, f32[3,2,256]{2,1,0:T(2,128)}, f32[2]{0:T(128)}) custom-call(f32[3,2,256]{2,1,0:T(2,128)} %bitcast.7, f32[3,2,256]{2,1,0:T(2,128)} %bitcast.8, f32[3,256]{1,0:T(4,128)} %first_end.1, f32[3,256]{1,0:T(4,128)} %last_end.1, s32[2,16,256]{2,1,0:T(8,128)} %nbr.1, s32[2,256]{1,0:T(2,128)} %cnt.1, ...), custom_call_target="tpu_custom_call" | custom-call | tf_op jit(solution)/shard_map/pallas_call | solution.py:674
  66.4 0.0 copy-start.2
  66.4 0.7 copy-done.2
  67.1 0.0 copy-start.1
  67.1 0.6 copy.24
  67.6 0.1 copy-done.1
  67.7 0.0 copy-start
  67.8 0.6 copy.25
  68.3 0.1 copy-done
  68.4 0.0 copy-start.3
  68.4 0.6 copy.26
  69.0 0.0 copy-done.3
  69.0 0.5 copy.27
Async XLA Ops:
  66.4 0.7 copy-start.2
  67.1 0.7 %copy-start.1 = (f32[3,2,256]{2,1,0:T(2,128)S(1)}, f32[3,2,256]{2,1,0:T(2,128)}, u32[]{:S(2)}) copy-start(f32[3,2,256]{2,1,0:T(2,128)} %get-tuple-element.9) | copy-start | bytes 18436
  67.7 0.7 %copy-start = (f32[3,2,256]{2,1,0:T(2,128)S(1)}, f32[3,2,256]{2,1,0:T(2,128)}, u32[]{:S(2)}) copy-start(f32[3,2,256]{2,1,0:T(2,128)} %get-tuple-element.10) | copy-start | bytes 18436
  68.4 0.6 copy-start.3

commit v3 on v2

--- a/solution.py
+++ b/solution.py
@@ -220,7 +220,7 @@
         mid, lo = pieces(rest)
         rcol[j] = nt(unit, hi.astype(b16)) + nt(unit, mid.astype(b16)) + nt(unit, lo.astype(b16))
 
-    group = 4 if slots % 4 == 0 else 1
+    group = math.gcd(slots, 8)
     pair = 2 if slots % 2 == 0 else 1
     centre = 0.5 * lax.broadcasted_iota(jnp.int32, (nb, group * atoms), 0).astype(f32)
 
@@ -263,7 +263,7 @@
         h1, l1 = pieces(inv1)
         h2, l2 = pieces(inv2)
         pre = nn(wmf[...], rows(h0, h1, h2, l0, l1, l2, h0, h1, h2))
-        sig = 1.0 / (1.0 + jnp.exp(-pre))
+        sig = 0.5 + 0.5 * jnp.tanh(0.5 * pre)
         return pre * sig, sig * (1.0 + pre * (1.0 - sig))
 
     def unmixed(mom, wmb, dpre):
@@ -327,7 +327,7 @@
             gap = wide([geo[i, 3, pl.ds(k, 1), :] for k in ks]) - centre
             hi, lo = pieces(jnp.exp(-2.0 * gap * gap))
             z = nn(wa_f[...], rows(hi, lo, hi, lo))
-            sig = 1.0 / (1.0 + jnp.exp(-z))
+            sig = 0.5 + 0.5 * jnp.tanh(0.5 * z)
             h = z * sig
             slope = sig * (1.0 + z * (1.0 - sig))
             hh, hl = pieces(h)

time: 69.9 us -> 66.5 us (0.951)
  Pallas kernels: 65.1 us -> 61.7 us
    pallas_call x1, Pallas kernels: 65.1 us -> 61.7 us  [local(): pl.pallas_call(functools.partial(kernel, n_image, n_space), out_shape=[st...]
where the time goes in v3:
time: 66.5 us; the launch traced here: 66.2 us
  Pallas kernels  61.7 us (93%)
  local copies, waits for them, and re-layouts  3.18 us (5%)
  between operations  1.3 us (2%)
    pallas_call x1, Pallas kernels, local(): pl.pallas_call(functools.partial(kernel, n_image, n_space), out_shape=[st...  61.7 us
    unnamed x12, local copies, waits for them, and re-layouts  3.18 us

profile of v3, /device:TPU:0, one launch (start us, length us, event | category | flops | bytes accessed | tf_op | source)
XLA Modules:
  0.0 66.2 jit_solution(8799028399123423625)
XLA Ops:
  1.3 61.7 %shard_map.174 = (f32[3,2,256]{2,1,0:T(2,128)}, f32[3,2,256]{2,1,0:T(2,128)}, f32[3,2,256]{2,1,0:T(2,128)}, f32[2]{0:T(128)}) custom-call(f32[3,2,256]{2,1,0:T(2,128)} %bitcast.7, f32[3,2,256]{2,1,0:T(2,128)} %bitcast.8, f32[3,256]{1,0:T(4,128)} %first_end.1, f32[3,256]{1,0:T(4,128)} %last_end.1, s32[2,16,256]{2,1,0:T(8,128)} %nbr.1, s32[2,256]{1,0:T(2,128)} %cnt.1, ...), custom_call_target="tpu_custom_call" | custom-call | tf_op jit(solution)/shard_map/pallas_call | solution.py:674
  63.0 0.0 copy-start.2
  63.0 0.7 %copy-done.2 = f32[3,2,256]{2,1,0:T(2,128)S(1)} copy-done((f32[3,2,256]{2,1,0:T(2,128)S(1)}, f32[3,2,256]{2,1,0:T(2,128)}, u32[]{:S(2)}) %copy-start.2) | copy-done | bytes 6168
  63.6 0.0 copy-start.1
  63.7 0.6 copy.24
  64.2 0.1 copy-done.1
  64.3 0.0 copy-start
  64.3 0.6 copy.25
  64.9 0.1 copy-done
  65.0 0.0 copy-start.3
  65.0 0.6 copy.26
  65.6 0.0 copy-done.3
  65.6 0.5 copy.27
Async XLA Ops:
  63.0 0.7 %copy-start.2 = (f32[3,2,256]{2,1,0:T(2,128)S(1)}, f32[3,2,256]{2,1,0:T(2,128)}, u32[]{:S(2)}) copy-start(f32[3,2,256]{2,1,0:T(2,128)} %get-tuple-element.8) | copy-start | bytes 18436
  63.6 0.7 %copy-start.1 = (f32[3,2,256]{2,1,0:T(2,128)S(1)}, f32[3,2,256]{2,1,0:T(2,128)}, u32[]{:S(2)}) copy-start(f32[3,2,256]{2,1,0:T(2,128)} %get-tuple-element.9) | copy-start | bytes 18436
  64.3 0.7 %copy-start = (f32[3,2,256]{2,1,0:T(2,128)S(1)}, f32[3,2,256]{2,1,0:T(2,128)}, u32[]{:S(2)}) copy-start(f32[3,2,256]{2,1,0:T(2,128)} %get-tuple-element.10) | copy-start | bytes 18436
  65.0 0.6 copy-start.3
